TPU v7x, 256 devices: a whole 4x4x8 slice. The times are simulated.
256 devices in a mesh: lat: 8 (over y, x_hi), lon: 32 (over z, x_lo, core).
Axes of the slice: x: 4 (x_hi: 2, x_lo: 2; x = x_hi * 2 + x_lo), y: 4, z: 8, core: 2. Of those that a mesh axis runs over, the one named last changes fastest.
Arguments:
- features: bfloat16 [4, 192, 384, 512], P(None, 'lat', 'lon'), may hold values from -6 to 6
- packed_first: bfloat16 [512, 1536], replicated, may hold values from -0.25 to 0.25
- scale_first: float32 [8], replicated, may hold values from 2 to 16
- output_first: bfloat16 [512, 512], replicated, may hold values from -0.25 to 0.25
- gain_first: float32 [512], replicated, may hold values from 0.5 to 1.5
- offset_first: float32 [512], replicated, may hold values from -1.5 to 1.5
- merge_weight: bfloat16 [2048, 1024], replicated, may hold values from -0.125 to 0.125
- merge_gain: float32 [1024], replicated, may hold values from 0.5 to 1.5
- merge_offset: float32 [1024], replicated, may hold values from -1.5 to 1.5
- packed_second: bfloat16 [1024, 1536], replicated, may hold values from -0.1875 to 0.1875
- scale_second: float32 [8], replicated, may hold values from 2 to 16
- output_second: bfloat16 [512, 1024], replicated, may hold values from -0.25 to 0.25
- gain_second: float32 [1024], replicated, may hold values from 0.5 to 1.5
- offset_second: float32 [1024], replicated, may hold values from -1.5 to 1.5
Outputs:
- coarse_out: bfloat16 [96, 32, 2, 12, 1024], P('lat', 'lon')
All inputs are finite; a program needn't handle non-finite values.
Results may differ from a plain program's by a relative error of at most 0.019.
Values may be sent and summed in bfloat16 or wider, within the bound.
A program may use at most 128 MiB of HBM per device.

v0:
```python
import jax
import jax.numpy as jnp
from jax import lax
from jax.sharding import PartitionSpec as P

WLEV = 2
WLAT = 6
WLON = 12


norm_eps = 1e-05
unit_eps = 1e-06


def passed_along(value, axis, by):
    devices = lax.axis_size(axis)
    return lax.ppermute(value, axis, [(i, (i + by) % devices) for i in range(devices)])


def from_partner(value, axis, distance):
    return lax.ppermute(value, axis, [(i, i ^ 1 << distance) for i in range(lax.axis_size(axis))])


def layer_norm(values, norm_gain, offset):
    average = jnp.mean(values, axis=-1, keepdims=True)
    centred = values - average
    spread = jnp.mean(centred * centred, axis=-1, keepdims=True)
    return centred * lax.rsqrt(spread + norm_eps) * norm_gain + offset


def unit_heads(tensor_in, head_count):
    shaped = tensor_in.reshape(
        tensor_in.shape[:-1] + (head_count, tensor_in.shape[-1] // head_count)
    ).astype(jnp.float32)
    scaled = shaped * lax.rsqrt(jnp.sum(shaped * shaped, axis=-1, keepdims=True) + unit_eps)
    return scaled.astype(jnp.bfloat16)


def attend(queries, keys_in, values_in, query_region, key_region, scales):
    head_count = scales.shape[0]
    query_unit = unit_heads(queries, head_count)
    key_unit = unit_heads(keys_in, head_count)
    scores = jnp.einsum("nahd,nbhd->nhab", query_unit, key_unit, preferred_element_type=jnp.float32)
    scores = scores * scales[None, :, None, None]
    allowed = (query_region[:, :, None] == key_region[:, None, :])[:, None]
    weights = jnp.where(allowed, jnp.exp(scores), jnp.zeros_like(scores))
    totals = jnp.sum(weights, axis=-1)
    value_heads = values_in.reshape(
        values_in.shape[:-1] + (head_count, values_in.shape[-1] // head_count)
    )
    mixture = jnp.einsum(
        "nhab,nbhd->nahd",
        weights.astype(jnp.bfloat16),
        value_heads,
        preferred_element_type=jnp.float32,
    )
    mixture = mixture / jnp.transpose(totals, (0, 2, 1))[..., None]
    return mixture.reshape(queries.shape).astype(jnp.bfloat16)


def to_windows(flat_tile, col_count):
    levels, row_count, joined = flat_tile.shape
    shaped = flat_tile.reshape(levels // WLEV, WLEV, row_count // WLAT, WLAT, joined)
    shaped = jnp.transpose(shaped, (0, 2, 1, 3, 4))
    return shaped.reshape(
        levels // WLEV * (row_count // WLAT), WLEV * WLAT * col_count, joined // col_count
    )


def from_windows(windows, levels, row_count):
    count, tokens, width = windows.shape
    col_count = tokens // (WLEV * WLAT)
    shaped = windows.reshape(levels // WLEV, row_count // WLAT, WLEV, WLAT, col_count * width)
    shaped = jnp.transpose(shaped, (0, 2, 1, 3, 4))
    return shaped.reshape(levels, row_count, col_count * width)


def lat_rows(row_count, lat_pos, lat_total):
    row_index = lat_pos * row_count + jnp.arange(row_count, dtype=jnp.int32)
    return (row_index >= lat_total - WLAT // 2).astype(jnp.int32)


def window_regions(level_wrapped, row_wrapped, col_count):
    levels = level_wrapped.shape[0]
    row_count = row_wrapped.shape[0]
    region = 2 * row_wrapped[None, :] + level_wrapped.astype(jnp.int32)[:, None]
    region = region.reshape(levels // WLEV, WLEV, row_count // WLAT, WLAT)
    region = jnp.transpose(region, (0, 2, 1, 3)).reshape(-1, WLEV * WLAT, 1)
    region = jnp.broadcast_to(region, (region.shape[0], WLEV * WLAT, col_count))
    return region.reshape(region.shape[0], WLEV * WLAT * col_count)


def project(windows, weight):
    product = jnp.dot(
        windows.reshape(-1, windows.shape[-1]), weight, preferred_element_type=jnp.float32
    )
    return product.astype(jnp.bfloat16).reshape(windows.shape[:-1] + (weight.shape[1],))


def finish(context, residual, output_weight, norm_gain, offset):
    width = output_weight.shape[0]
    projected = jnp.dot(
        context.reshape(-1, width), output_weight, preferred_element_type=jnp.float32
    )
    branch = layer_norm(projected, norm_gain, offset).reshape(residual.shape)
    return (residual.astype(jnp.float32) + branch).astype(jnp.bfloat16)


def body(
    features,
    packed_first,
    scale_first,
    output_first,
    gain_first,
    offset_first,
    merge_weight,
    merge_gain,
    merge_offset,
    packed_second,
    scale_second,
    output_second,
    gain_second,
    offset_second,
):
    levels, row_count, col_count, channels = features.shape
    lat_total = row_count * lax.axis_size("lat")
    lat_pos = lax.axis_index("lat")
    lon_pos = lax.axis_index("lon")
    half_lat = WLAT // 2
    half_lon = WLON // 2
    inner_width = packed_first.shape[1] // 3
    query_weight = packed_first[:, :inner_width]
    pair_weight = packed_first[:, inner_width:]
    flat_grid = features.reshape(levels, row_count, col_count * channels)
    rim_rows = passed_along(flat_grid[:, :half_lat], "lat", -1)
    rolled = jnp.concatenate([flat_grid[:, half_lat:], rim_rows], axis=1)
    rolled = jnp.concatenate([rolled[WLEV // 2 :], rolled[: WLEV // 2]], axis=0)
    level_wrapped = jnp.arange(levels) >= levels - WLEV // 2
    row_wrapped = lat_rows(row_count, lat_pos, lat_total)
    split_in = half_lon * channels
    split_out = half_lon * inner_width
    incoming = passed_along(rolled[:, :, :split_in], "lon", -1)
    tile_grid = jnp.concatenate([rolled[:, :, split_in:], incoming], axis=2)
    windows = to_windows(tile_grid, col_count)
    region = window_regions(level_wrapped, row_wrapped, col_count)
    queries = project(windows, query_weight)
    pairs = project(windows, pair_weight)
    context = attend(
        queries, pairs[..., :inner_width], pairs[..., inner_width:], region, region, scale_first
    )
    context = from_windows(context, levels, row_count)
    returned = passed_along(context[:, :, split_out:], "lon", 1)
    context = jnp.concatenate([returned, context[:, :, :split_out]], axis=2)
    context = jnp.concatenate(
        [context[levels - WLEV // 2 :], context[: levels - WLEV // 2]], axis=0
    )
    returned = passed_along(context[:, row_count - half_lat :], "lat", 1)
    context = jnp.concatenate([returned, context[:, : row_count - half_lat]], axis=1)
    first_out = finish(context, features, output_first, gain_first, offset_first)
    half_rows = row_count // 2
    half_cols = col_count // 2
    pair_rows = first_out.reshape(levels, half_rows, 2, half_cols, 2 * channels)
    merge_total = None
    for parity in range(2):
        stacked = jnp.concatenate(
            [
                merge_weight[parity * channels : (parity + 1) * channels],
                merge_weight[(2 + parity) * channels : (3 + parity) * channels],
            ],
            axis=0,
        )
        term = jnp.dot(
            pair_rows[:, :, parity].reshape(-1, 2 * channels),
            stacked,
            preferred_element_type=jnp.float32,
        )
        merge_total = term if merge_total is None else merge_total + term
    merged = layer_norm(merge_total, merge_gain, merge_offset).astype(jnp.bfloat16)
    wide = merged.shape[-1]
    merged = merged.reshape(levels, half_rows, half_cols * wide)
    is_even = lon_pos % 2 == 0
    outgoing = jnp.where(is_even, merged[WLEV:], merged[:WLEV])
    keep_part = jnp.where(is_even, merged[:WLEV], merged[WLEV:])
    incoming = from_partner(outgoing, "lon", 0)
    own_levels = jnp.where(
        is_even,
        jnp.concatenate([keep_part, incoming], axis=2),
        jnp.concatenate([incoming, keep_part], axis=2),
    )
    level_edge = from_partner(own_levels[:1], "lon", 0)
    rolled = jnp.concatenate([own_levels[1:], level_edge], axis=0)
    rim_rows = passed_along(rolled[:, :half_lat], "lat", -1)
    rolled = jnp.concatenate([rolled[:, half_lat:], rim_rows], axis=1)
    split_wide = half_lon * wide
    incoming = passed_along(rolled[:, :, :split_wide], "lon", -2)
    tile_grid = jnp.concatenate([rolled[:, :, split_wide:], incoming], axis=2)
    second_width = packed_second.shape[1] // 3
    level_wrapped = jnp.logical_and(jnp.arange(WLEV) == WLEV - 1, jnp.logical_not(is_even))
    row_wrapped = lat_rows(half_rows, lat_pos, lat_total // 2)
    region = window_regions(level_wrapped, row_wrapped, WLON)
    windows = to_windows(tile_grid, WLON)
    queries = project(windows, packed_second[:, :second_width])
    pairs = project(windows, packed_second[:, second_width:])
    context = attend(
        queries, pairs[..., :second_width], pairs[..., second_width:], region, region, scale_second
    )
    context = from_windows(context, WLEV, half_rows)
    split_back = half_lon * second_width
    returned = passed_along(context[:, :, split_back:], "lon", 2)
    context = jnp.concatenate([returned, context[:, :, :split_back]], axis=2)
    returned = passed_along(context[:, half_rows - half_lat :], "lat", 1)
    context = jnp.concatenate([returned, context[:, : half_rows - half_lat]], axis=1)
    returned = from_partner(context[1:], "lon", 0)
    context = jnp.concatenate([returned, context[:1]], axis=0)
    second = finish(
        context,
        own_levels.reshape(WLEV, half_rows, WLON, wide),
        output_second,
        gain_second,
        offset_second,
    )
    return jnp.transpose(second, (1, 0, 2, 3))[:, None]


def solution(mesh):
    return jax.shard_map(
        body,
        mesh=mesh,
        in_specs=(
            P(None, "lat", "lon", None),
            P(),
            P(),
            P(),
            P(),
            P(),
            P(),
            P(),
            P(),
            P(),
            P(),
            P(),
            P(),
            P(),
        ),
        out_specs=P("lat", "lon", None, None, None),
        check_vma=False,
    )
```

profile of v0, /device:TPU:1, one launch (start us, length us, event | category | flops | bytes accessed | tf_op | source)
XLA Modules:
  0.0 200.0 jit_solution(138362689104837247)
XLA Ops:
  0.0 1.4 copy.167
  1.5 6.1 %collective-permute-start = (bf16[4,3,6144]{2,1,0:T(4,128)(2,1)S(1)}, bf16[4,3,6144]{2,1,0:T(4,128)(2,1)S(1)}, u32[]{:S(2)}, u32[]{:S(2)}) collective-permute-start(bf16[4,3,6144]{2,1,0:T(4,128)(2,1)S(1)} %slice.165), channel_id=1, source_target_pairs={{0,224},{32,0},{64,32},{96,64},{128,96},{160,128},{192,160},{224,1... | collective-permute-start | bytes 442376 | tf_op jit(solution)/shard_map/ppermute | solution.py:17
  7.9 3.3 %collective-permute-done = bf16[4,3,6144]{2,1,0:T(4,128)(2,1)S(1)} collective-permute-done((bf16[4,3,6144]{2,1,0:T(4,128)(2,1)S(1)}, bf16[4,3,6144]{2,1,0:T(4,128)(2,1)S(1)}, u32[]{:S(2)}, u32[]{:S(2)}) %collective-permute-start) | collective-permute-done | bytes 147488 | tf_op jit(solution)/shard_map/ppermute | solution.py:17
  11.5 1.6 collective-permute-start.1
  14.4 6.5 %collective-permute-done.1 = bf16[4,24,3072]{2,1,0:T(8,128)(2,1)S(1)} collective-permute-done((bf16[4,24,3072]{2,1,0:T(8,128)(2,1)S(1)}, bf16[4,24,3072]{2,1,0:T(8,128)(2,1)S(1)}, u32[]{:S(2)}, u32[]{:S(2)}) %collective-permute-start.1) | collective-permute-done | bytes 589856 | tf_op jit(solution)/shard_map/ppermute | solution.py:17
  21.9 2.0 reshape.222
  23.9 1.9 copy.138
  25.8 2.3 %reshape_reshape.4 = bf16[1152,512]{1,0:T(8,128)(2,1)} reshape(bf16[2,4,2,6,6144]{4,3,2,1,0:T(8,128)(2,1)S(1)} %copy.138) | data formatting | bytes 2359296 | tf_op jit(solution)/shard_map/reshape;reshape | solution.py:95
  28.1 3.8 %fusion.8 = f32[1152,512]{1,0:T(8,128)} fusion(bf16[1152,512]{1,0:T(8,128)(2,1)} %reshape_reshape.4, bf16[512,1536]{1,0:T(8,128)(2,1)} %param.15), kind=kOutput, calls=%fused_computation.16 | convolution fusion | flops 605159424 | bytes 4063232 | tf_op jit(solution)/shard_map/dot_general | solution.py:94
  31.9 2.8 %convolution_convert_fusion = bf16[1152,1024]{1,0:T(8,128)(2,1)} fusion(bf16[1152,512]{1,0:T(8,128)(2,1)S(1)} %copy-done.3, bf16[512,1536]{1,0:T(8,128)(2,1)S(1)} %copy-done.17), kind=kOutput, calls=%fused_computation.13 | convolution fusion | flops 1209139200 | bytes 4587520 | tf_op jit(solution)/shard_map/dot_general | solution.py:94
  34.6 2.0 %copy.140 = f32[1152,512]{0,1:T(8,128)S(1)} copy(f32[1152,512]{1,0:T(8,128)} %fusion.8) | data formatting | bytes 4718592 | tf_op jit(solution)/shard_map/convert_element_type | solution.py:34
  36.7 4.1 %reshape.235 = f32[8,144,8,64]{1,0,3,2:T(8,128)} reshape(f32[1152,512]{0,1:T(8,128)S(1)} %copy.140) | data formatting | bytes 4718592 | tf_op jit(solution)/shard_map/convert_element_type | solution.py:34
  40.8 2.7 %multiply_reduce_fusion.1 = f32[8,144,8]{1,0,2:T(8,128)S(1)} fusion(f32[8,144,8,64]{1,0,3,2:T(8,128)} %reshape.235), kind=kLoop, calls=%fused_computation.12 | loop fusion | flops 1170432 | bytes 2396160 | tf_op jit(solution)/shard_map/reduce_sum | solution.py:35
  44.2 1.7 multiply_convert_fusion.1
  46.6 1.5 slice_convert_fusion
  48.1 3.3 %copy.141 = f32[8,144,512]{1,2,0:T(8,128)} copy(f32[8,144,512]{2,1,0:T(8,128)S(1)} %get-tuple-element.9) | data formatting | bytes 4718592 | tf_op jit(solution)/shard_map/convert_element_type | solution.py:34
  51.4 2.8 %multiply_reduce_fusion = f32[8,144,8]{1,2,0:T(8,128)S(1)} fusion(f32[8,144,512]{1,2,0:T(8,128)} %copy.141), kind=kLoop, calls=%fused_computation.10 | loop fusion | flops 1170432 | bytes 2396160 | tf_op jit(solution)/shard_map/reduce_sum | solution.py:35
  54.4 3.7 %copy.139 = bf16[8,144,512]{1,2,0:T(8,128)(2,1)} copy(bf16[8,144,512]{2,1,0:T(8,128)(2,1)} %get-tuple-element.10) | data formatting | bytes 2359296 | tf_op jit(solution)/shard_map/slice | solution.py:149
  58.2 4.8 %fusion = (f32[8,8,144]{2,1,0:T(8,128)S(1)}, f32[8,8,144,144]{2,3,1,0:T(8,128)S(1)}) fusion(f32[8]{0:T(128)S(1)} %copy-done.24, pred[8,144,144]{1,2,0:T(8,128)(4,1)S(1)} %copy-done.8, f32[8,144,8,64]{1,3,2,0:T(8,128)} %bitcast.57, f32[8,144,8]{1,2,0:T(8,128)S(1)} %copy.143, bf16[8,144,8,64]{1,0,3,2:T(8,128)(2,1)S(1)} %copy-done.2), kind=kOutput, calls=%fused_computation.1 | convolution fusion | flops 175021056 | bytes 9087008 | tf_op jit(solution)/shard_map/nahd,nbhd->nhab/dot_general | solution.py:43
  63.0 3.2 %fusion.7 = bf16[8,144,8,64]{1,3,2,0:T(8,128)(2,1)} fusion(bf16[8,144,8,64]{1,3,2,0:T(8,128)(2,1)S(1)} %bitcast.66, f32[8,8,144,144]{2,3,1,0:T(8,128)S(1)} %get-tuple-element.30, f32[8]{0:T(128)S(1)} %copy-done.24, pred[8,144,144]{1,2,0:T(8,128)(4,1)S(1)} %copy-done.8, f32[8,144,8]{1,2,0:T(8,128)S(1)} %bitcast.71), kind=kOutput, calls=%fused_computation.8 | convolution fusion | flops 175030272 | bytes 7870496 | tf_op jit(solution)/shard_map/nhab,nbhd->nahd/dot_general | solution.py:51
  66.2 3.2 %copy.146 = bf16[8,144,8,64]{3,2,1,0:T(8,128)(2,1)S(1)} copy(bf16[8,144,8,64]{1,3,2,0:T(8,128)(2,1)} %fusion.7) | data formatting | bytes 2359296 | tf_op jit(solution)/shard_map/convert_element_type | solution.py:58
  69.4 2.9 %convert_element_type.119 = bf16[2,4,2,6,6144]{4,3,2,1,0:T(8,128)(2,1)} reshape(bf16[8,144,8,64]{3,2,1,0:T(8,128)(2,1)S(1)} %copy.146) | data formatting | bytes 2359296 | tf_op jit(solution)/shard_map/convert_element_type | solution.py:58
  72.3 3.6 %copy.147 = bf16[2,2,4,6,6144]{4,1,0,3,2:T(2,128)(2,1)} copy(bf16[2,2,4,6,6144]{4,3,1,2,0:T(8,128)(2,1)} %bitcast.59) | data formatting | bytes 2359296 | tf_op jit(solution)/shard_map/transpose | solution.py:74
  75.9 3.3 %reshape.225 = bf16[4,24,6144]{2,0,1:T(4,128)(2,1)S(1)} reshape(bf16[2,2,4,6,6144]{4,1,0,3,2:T(2,128)(2,1)} %copy.147) | data formatting | bytes 2359296 | tf_op jit(solution)/shard_map/reshape | solution.py:75
  79.8 6.8 %collective-permute-done.2 = bf16[4,24,3072]{2,0,1:T(4,128)(2,1)S(1)} collective-permute-done((bf16[4,24,3072]{2,0,1:T(4,128)(2,1)S(1)}, bf16[4,24,3072]{2,0,1:T(4,128)(2,1)S(1)}, u32[]{:S(2)}, u32[]{:S(2)}) %collective-permute-start.2) | collective-permute-done | bytes 589856 | tf_op jit(solution)/shard_map/ppermute | solution.py:17
  87.5 2.8 %collective-permute-start.3 = (bf16[4,3,6144]{2,0,1:T(4,128)(2,1)S(1)}, bf16[4,3,6144]{2,0,1:T(4,128)(2,1)S(1)}, u32[]{:S(2)}, u32[]{:S(2)}) collective-permute-start(bf16[4,3,6144]{2,0,1:T(4,128)(2,1)S(1)} %pad_maximum_fusion.9), channel_id=1, source_target_pairs={{0,32},{32,64},{64,96},{96,128},{128,160},{160,192},{192,224},{224... | collective-permute-start | bytes 442376 | tf_op jit(solution)/shard_map/ppermute | solution.py:17
  90.4 2.0 %fusion.58 = (bf16[512,1024]{1,0:T(8,128)(2,1)}, bf16[512,1024]{1,0:T(8,128)(2,1)}, bf16[512,1024]{1,0:T(8,128)(2,1)}, bf16[512,1024]{1,0:T(8,128)(2,1)}) fusion(bf16[2048,1024]{1,0:T(8,128)(2,1)S(1)} %copy-done.4), kind=kLoop, calls=%fused_computation.115 | loop fusion | bytes 8388608 | tf_op jit(solution)/shard_map/slice | solution.py:167
  92.4 4.1 %collective-permute-done.3 = bf16[4,3,6144]{2,0,1:T(4,128)(2,1)S(1)} collective-permute-done((bf16[4,3,6144]{2,0,1:T(4,128)(2,1)S(1)}, bf16[4,3,6144]{2,0,1:T(4,128)(2,1)S(1)}, u32[]{:S(2)}, u32[]{:S(2)}) %collective-permute-start.3) | collective-permute-done | bytes 147488 | tf_op jit(solution)/shard_map/ppermute | solution.py:17
  98.3 1.5 reshape.226
  99.9 1.9 fusion.65
  102.9 1.8 reshape.227
  104.7 4.1 %add_convert_fusion = bf16[4,24,12,512]{3,2,1,0:T(8,128)(2,1)} fusion(f32[4,24,12,512]{3,2,1,0:T(8,128)} %reshape.227, bf16[4,24,12,512]{3,1,2,0:T(8,128)(2,1)} %param.14), kind=kLoop, calls=%fused_computation.14 | loop fusion | flops 1769472 | bytes 4718592 | tf_op jit(solution)/shard_map/convert_element_type | solution.py:106
  108.9 2.4 %reshape.228 = bf16[4,12,2,6,1024]{4,3,2,1,0:T(8,128)(2,1)S(1)} reshape(bf16[4,24,12,512]{3,2,1,0:T(8,128)(2,1)} %add_convert_fusion) | data formatting | bytes 2359296 | tf_op jit(solution)/shard_map/reshape | solution.py:162
  112.3 2.1 %reshape_squeeze.6 = bf16[288,1024]{1,0:T(8,128)(2,1)} reshape(bf16[4,12,1,6,1024]{4,3,2,1,0:T(8,128)(2,1)} %get-tuple-element.12) | data formatting | bytes 1179648 | tf_op jit(solution)/shard_map/reshape;squeeze | solution.py:173
  115.5 2.3 %fusion.12 = f32[288,1024]{1,0:T(8,128)S(1)} fusion(bf16[288,1024]{1,0:T(8,128)(2,1)} %reshape_squeeze.6, bf16[512,1024]{1,0:T(8,128)(2,1)S(1)} %copy-done.11, bf16[512,1024]{1,0:T(8,128)(2,1)} %get-tuple-element.7), kind=kOutput, calls=%fused_computation.21 | convolution fusion | flops 608174080 | bytes 3866624 | tf_op jit(solution)/shard_map/dot_general | solution.py:172
  119.7 9.9 %collective-permute-start.4 = (bf16[2,12,6144]{2,1,0:T(8,128)(2,1)S(1)}, bf16[2,12,6144]{2,1,0:T(8,128)(2,1)S(1)}, u32[]{:S(2)}, u32[]{:S(2)}) collective-permute-start(bf16[2,12,6144]{2,1,0:T(8,128)(2,1)S(1)} %select_n.57), channel_id=1, source_target_pairs={{0,1},{1,0},{2,3},{3,2},{4,5},{5,4},{6,7},{7,6},{8,9},{9,8},{10,11... | collective-permute-start | bytes 884744 | tf_op jit(solution)/shard_map/ppermute | solution.py:21
  133.2 3.3 %collective-permute-start.6 = (bf16[2,3,12288]{2,1,0:T(4,128)(2,1)S(1)}, bf16[2,3,12288]{2,1,0:T(4,128)(2,1)S(1)}, u32[]{:S(2)}, u32[]{:S(2)}) collective-permute-start(bf16[2,3,12288]{2,1,0:T(4,128)(2,1)S(1)} %pad_maximum_fusion.8), channel_id=1, source_target_pairs={{0,224},{32,0},{64,32},{96,64},{128,96},{160,128},{192,160},{224,1... | collective-permute-start | bytes 442376 | tf_op jit(solution)/shard_map/ppermute | solution.py:17
  136.7 4.1 %collective-permute-done.6 = bf16[2,3,12288]{2,1,0:T(4,128)(2,1)S(1)} collective-permute-done((bf16[2,3,12288]{2,1,0:T(4,128)(2,1)S(1)}, bf16[2,3,12288]{2,1,0:T(4,128)(2,1)S(1)}, u32[]{:S(2)}, u32[]{:S(2)}) %collective-permute-start.6) | collective-permute-done | bytes 147488 | tf_op jit(solution)/shard_map/ppermute | solution.py:17
  142.4 5.8 %collective-permute-done.7 = bf16[2,12,6144]{2,1,0:T(8,128)(2,1)S(1)} collective-permute-done((bf16[2,12,6144]{2,1,0:T(8,128)(2,1)S(1)}, bf16[2,12,6144]{2,1,0:T(8,128)(2,1)S(1)}, u32[]{:S(2)}, u32[]{:S(2)}) %collective-permute-start.7) | collective-permute-done | bytes 294944 | tf_op jit(solution)/shard_map/ppermute | solution.py:17
  149.3 1.7 reshape_reshape.5
  151.0 1.9 fusion.34
  152.9 3.2 %fusion.30 = bf16[288,1024]{1,0:T(8,128)(2,1)} fusion(bf16[288,1024]{1,0:T(8,128)(2,1)S(1)} %copy-done.14, bf16[1024,1536]{1,0:T(8,128)(2,1)} %param.23), kind=kOutput, calls=%fused_computation.39 | convolution fusion | flops 604274688 | bytes 3276800 | tf_op jit(solution)/shard_map/dot_general | solution.py:94
  160.7 2.0 fusion.24
  164.7 1.6 collective-permute-start.8
  166.3 4.6 %collective-permute-done.8 = bf16[2,12,3072]{2,0,1:T(2,128)(2,1)S(1)} collective-permute-done((bf16[2,12,3072]{2,0,1:T(2,128)(2,1)S(1)}, bf16[2,12,3072]{2,0,1:T(2,128)(2,1)S(1)}, u32[]{:S(2)}, u32[]{:S(2)}) %collective-permute-start.8) | collective-permute-done | bytes 147488 | tf_op jit(solution)/shard_map/ppermute | solution.py:17
  171.5 6.6 %collective-permute-done.9 = bf16[2,3,6144]{2,0,1:T(2,128)(2,1)S(1)} collective-permute-done((bf16[2,3,6144]{2,0,1:T(2,128)(2,1)S(1)}, bf16[2,3,6144]{2,0,1:T(2,128)(2,1)S(1)}, u32[]{:S(2)}, u32[]{:S(2)}) %collective-permute-start.9) | collective-permute-done | bytes 73760 | tf_op jit(solution)/shard_map/ppermute | solution.py:17
  178.8 12.9 %collective-permute-start.10 = (bf16[1,12,6144]{2,0,1:T(2,128)(2,1)S(1)}, bf16[1,12,6144]{2,0,1:T(2,128)(2,1)S(1)}, u32[]{:S(2)}, u32[]{:S(2)}) collective-permute-start(bf16[1,12,6144]{2,0,1:T(2,128)(2,1)S(1)} %get-tuple-element.25), channel_id=1, source_target_pairs={{0,1},{1,0},{2,3},{3,2},{4,5},{5,4},{6,7},{7,6},{8,9},{9,8},{10,11... | collective-permute-start | bytes 442376 | tf_op jit(solution)/shard_map/ppermute | solution.py:21
  198.3 1.4 copy.163
  (141 shorter events, 33.2 us)
Async XLA Ops:
  0.0 194.2 %copy-start = (bf16[512,1024]{1,0:T(8,128)(2,1)S(1)}, bf16[512,1024]{1,0:T(8,128)(2,1)}, u32[]{:S(2)}) copy-start(bf16[512,1024]{1,0:T(8,128)(2,1)} %param.25) | copy-start | bytes 3145732
  1.5 9.7 %collective-permute-start = (bf16[4,3,6144]{2,1,0:T(4,128)(2,1)S(1)}, bf16[4,3,6144]{2,1,0:T(4,128)(2,1)S(1)}, u32[]{:S(2)}, u32[]{:S(2)}) collective-permute-start(bf16[4,3,6144]{2,1,0:T(4,128)(2,1)S(1)} %slice.165), channel_id=1, source_target_pairs={{0,224},{32,0},{64,32},{96,64},{128,96},{160,128},{192,160},{224,1... | collective-permute-start | bytes 442376 | tf_op jit(solution)/shard_map/ppermute | solution.py:17
  11.5 9.4 %collective-permute-start.1 = (bf16[4,24,3072]{2,1,0:T(8,128)(2,1)S(1)}, bf16[4,24,3072]{2,1,0:T(8,128)(2,1)S(1)}, u32[]{:S(2)}, u32[]{:S(2)}) collective-permute-start(bf16[4,24,3072]{2,1,0:T(8,128)(2,1)S(1)} %get-tuple-element.16), channel_id=1, source_target_pairs={{0,31},{1,0},{2,1},{3,2},{4,3},{5,4},{6,5},{7,6},{8,7},{9,8},{10,9... | collective-permute-start | bytes 1769480 | tf_op jit(solution)/shard_map/ppermute | solution.py:17
  28.1 3.8 %copy-start.3 = (bf16[1152,512]{1,0:T(8,128)(2,1)S(1)}, bf16[1152,512]{1,0:T(8,128)(2,1)}, u32[]{:S(2)}) copy-start(bf16[1152,512]{1,0:T(8,128)(2,1)} %reshape_reshape.4) | copy-start | bytes 3538948
  28.1 3.8 %copy-start.17 = (bf16[512,1536]{1,0:T(8,128)(2,1)S(1)}, bf16[512,1536]{1,0:T(8,128)(2,1)}, u32[]{:S(2)}) copy-start(bf16[512,1536]{1,0:T(8,128)(2,1)} %param.15) | copy-start | bytes 4718596
  40.8 3.4 %copy-start.1 = (f32[8,144,8,64]{1,0,3,2:T(8,128)S(1)}, f32[8,144,8,64]{1,0,3,2:T(8,128)}, u32[]{:S(2)}) copy-start(f32[8,144,8,64]{1,0,3,2:T(8,128)} %reshape.235) | copy-start | bytes 7077892
  44.2 2.4 %copy-start.5 = (bf16[1152,1024]{1,0:T(8,128)(2,1)S(1)}, bf16[1152,1024]{1,0:T(8,128)(2,1)}, u32[]{:S(2)}) copy-start(bf16[1152,1024]{1,0:T(8,128)(2,1)} %convolution_convert_fusion) | copy-start | bytes 7077892
  54.3 3.9 %copy-start.2 = (bf16[8,144,8,64]{1,0,3,2:T(8,128)(2,1)S(1)}, bf16[8,144,8,64]{1,0,3,2:T(8,128)(2,1)}, u32[]{:S(2)}) copy-start(bf16[8,144,8,64]{1,0,3,2:T(8,128)(2,1)} %multiply_convert_fusion.1) | copy-start | bytes 3538948
  54.3 3.8 %copy-start.8 = (pred[8,144,144]{1,2,0:T(8,128)(4,1)S(1)}, pred[8,144,144]{1,2,0:T(8,128)(4,1)}, u32[]{:S(2)}) copy-start(pred[8,144,144]{1,2,0:T(8,128)(4,1)} %broadcast_compare_fusion) | copy-start | bytes 497668
  54.3 3.8 %copy-start.24 = (f32[8]{0:T(128)S(1)}, f32[8]{0:T(128)}, u32[]{:S(2)}) copy-start(f32[8]{0:T(128)} %param.16) | copy-start | bytes 100
  58.2 4.8 %copy-start.6 = (bf16[8,144,512]{1,2,0:T(8,128)(2,1)S(1)}, bf16[8,144,512]{1,2,0:T(8,128)(2,1)}, u32[]{:S(2)}) copy-start(bf16[8,144,512]{1,2,0:T(8,128)(2,1)} %copy.139) | copy-start | bytes 3538948
  79.2 11.1 %copy-start.4 = (bf16[2048,1024]{1,0:T(8,128)(2,1)S(1)}, bf16[2048,1024]{1,0:T(8,128)(2,1)}, u32[]{:S(2)}) copy-start(bf16[2048,1024]{1,0:T(8,128)(2,1)} %param.20) | copy-start | bytes 12582916
  79.7 6.9 %collective-permute-start.2 = (bf16[4,24,3072]{2,0,1:T(4,128)(2,1)S(1)}, bf16[4,24,3072]{2,0,1:T(4,128)(2,1)S(1)}, u32[]{:S(2)}, u32[]{:S(2)}) collective-permute-start(bf16[4,24,3072]{2,0,1:T(4,128)(2,1)S(1)} %get-tuple-element.14), channel_id=1, source_target_pairs={{0,1},{1,2},{2,3},{3,4},{4,5},{5,6},{6,7},{7,8},{8,9},{9,10},{10,1... | collective-permute-start | bytes 1769480 | tf_op jit(solution)/shard_map/ppermute | solution.py:17
  87.5 9.0 %collective-permute-start.3 = (bf16[4,3,6144]{2,0,1:T(4,128)(2,1)S(1)}, bf16[4,3,6144]{2,0,1:T(4,128)(2,1)S(1)}, u32[]{:S(2)}, u32[]{:S(2)}) collective-permute-start(bf16[4,3,6144]{2,0,1:T(4,128)(2,1)S(1)} %pad_maximum_fusion.9), channel_id=1, source_target_pairs={{0,32},{32,64},{64,96},{96,128},{128,160},{160,192},{192,224},{224... | collective-permute-start | bytes 442376 | tf_op jit(solution)/shard_map/ppermute | solution.py:17
  101.8 0.7 copy-start.22
  101.8 0.7 copy-start.23
  112.3 3.2 %copy-start.11 = (bf16[512,1024]{1,0:T(8,128)(2,1)S(1)}, bf16[512,1024]{1,0:T(8,128)(2,1)}, u32[]{:S(2)}) copy-start(bf16[512,1024]{1,0:T(8,128)(2,1)} %get-tuple-element.6) | copy-start | bytes 3145732
  115.5 2.3 %copy-start.9 = (bf16[512,1024]{1,0:T(8,128)(2,1)S(1)}, bf16[512,1024]{1,0:T(8,128)(2,1)}, u32[]{:S(2)}) copy-start(bf16[512,1024]{1,0:T(8,128)(2,1)} %get-tuple-element.5) | copy-start | bytes 3145732
  115.5 2.4 %copy-start.10 = (bf16[512,1024]{1,0:T(8,128)(2,1)S(1)}, bf16[512,1024]{1,0:T(8,128)(2,1)}, u32[]{:S(2)}) copy-start(bf16[512,1024]{1,0:T(8,128)(2,1)} %get-tuple-element.8) | copy-start | bytes 3145732
  115.5 2.4 %copy-start.13 = (bf16[288,1024]{1,0:T(8,128)(2,1)S(1)}, bf16[288,1024]{1,0:T(8,128)(2,1)}, u32[]{:S(2)}) copy-start(bf16[288,1024]{1,0:T(8,128)(2,1)} %reshape_squeeze.7) | copy-start | bytes 1769476
  117.9 1.2 copy-start.18
  117.9 1.2 copy-start.19
  119.7 11.2 %collective-permute-start.4 = (bf16[2,12,6144]{2,1,0:T(8,128)(2,1)S(1)}, bf16[2,12,6144]{2,1,0:T(8,128)(2,1)S(1)}, u32[]{:S(2)}, u32[]{:S(2)}) collective-permute-start(bf16[2,12,6144]{2,1,0:T(8,128)(2,1)S(1)} %select_n.57), channel_id=1, source_target_pairs={{0,1},{1,0},{2,3},{3,2},{4,5},{5,4},{6,7},{7,6},{8,9},{9,8},{10,11... | collective-permute-start | bytes 884744 | tf_op jit(solution)/shard_map/ppermute | solution.py:21
  131.3 1.8 collective-permute-start.5
  133.2 7.7 %collective-permute-start.6 = (bf16[2,3,12288]{2,1,0:T(4,128)(2,1)S(1)}, bf16[2,3,12288]{2,1,0:T(4,128)(2,1)S(1)}, u32[]{:S(2)}, u32[]{:S(2)}) collective-permute-start(bf16[2,3,12288]{2,1,0:T(4,128)(2,1)S(1)} %pad_maximum_fusion.8), channel_id=1, source_target_pairs={{0,224},{32,0},{64,32},{96,64},{128,96},{160,128},{192,160},{224,1... | collective-permute-start | bytes 442376 | tf_op jit(solution)/shard_map/ppermute | solution.py:17
  141.1 7.2 %collective-permute-start.7 = (bf16[2,12,6144]{2,1,0:T(8,128)(2,1)S(1)}, bf16[2,12,6144]{2,1,0:T(8,128)(2,1)S(1)}, u32[]{:S(2)}, u32[]{:S(2)}) collective-permute-start(bf16[2,12,6144]{2,1,0:T(8,128)(2,1)S(1)} %get-tuple-element.18), channel_id=1, source_target_pairs={{0,30},{1,31},{2,0},{3,1},{4,2},{5,3},{6,4},{7,5},{8,6},{9,7},{10,... | collective-permute-start | bytes 884744 | tf_op jit(solution)/shard_map/ppermute | solution.py:17
  151.0 1.9 copy-start.14
  157.0 1.2 copy-start.12
  159.0 1.7 copy-start.15
  159.0 1.7 copy-start.25
  160.7 2.0 %copy-start.16 = (pred[2,144,144]{1,2,0:T(8,128)(4,1)S(1)}, pred[2,144,144]{1,2,0:T(8,128)(4,1)}, u32[]{:S(2)}) copy-start(pred[2,144,144]{1,2,0:T(8,128)(4,1)} %broadcast_compare_fusion.1) | copy-start | bytes 124420
  164.7 6.2 %collective-permute-start.8 = (bf16[2,12,3072]{2,0,1:T(2,128)(2,1)S(1)}, bf16[2,12,3072]{2,0,1:T(2,128)(2,1)S(1)}, u32[]{:S(2)}, u32[]{:S(2)}) collective-permute-start(bf16[2,12,3072]{2,0,1:T(2,128)(2,1)S(1)} %get-tuple-element.27), channel_id=1, source_target_pairs={{0,2},{1,3},{2,4},{3,5},{4,6},{5,7},{6,8},{7,9},{8,10},{9,11},{10,... | collective-permute-start | bytes 442376 | tf_op jit(solution)/shard_map/ppermute | solution.py:17
  171.0 7.2 %collective-permute-start.9 = (bf16[2,3,6144]{2,0,1:T(2,128)(2,1)S(1)}, bf16[2,3,6144]{2,0,1:T(2,128)(2,1)S(1)}, u32[]{:S(2)}, u32[]{:S(2)}) collective-permute-start(bf16[2,3,6144]{2,0,1:T(2,128)(2,1)S(1)} %pad_maximum_fusion.10), channel_id=1, source_target_pairs={{0,32},{32,64},{64,96},{96,128},{128,160},{160,192},{192,224},{224... | collective-permute-start | bytes 221192 | tf_op jit(solution)/shard_map/ppermute | solution.py:17
  178.8 14.1 %collective-permute-start.10 = (bf16[1,12,6144]{2,0,1:T(2,128)(2,1)S(1)}, bf16[1,12,6144]{2,0,1:T(2,128)(2,1)S(1)}, u32[]{:S(2)}, u32[]{:S(2)}) collective-permute-start(bf16[1,12,6144]{2,0,1:T(2,128)(2,1)S(1)} %get-tuple-element.25), channel_id=1, source_target_pairs={{0,1},{1,0},{2,3},{3,2},{4,5},{5,4},{6,7},{7,6},{8,9},{9,8},{10,11... | collective-permute-start | bytes 442376 | tf_op jit(solution)/shard_map/ppermute | solution.py:21
  193.7 1.3 copy-start.20
  193.7 1.3 copy-start.21
  195.1 2.7 %copy-start.7 = (bf16[2,12,6,1024]{3,2,1,0:T(8,128)(2,1)S(1)}, bf16[2,12,6,1024]{3,2,1,0:T(8,128)(2,1)}, u32[]{:S(2)}) copy-start(bf16[2,12,6,1024]{3,2,1,0:T(8,128)(2,1)} %select_n.55) | copy-start | bytes 884740
where the time goes:
time: 204 us; the launch traced here: 200 us
  local copies, waits for them, and re-layouts  62.1 us (30%)
  waiting for transfers between devices  44.2 us (22%)
  starting transfers between devices  39.7 us (19%)
  matrix products  28 us (14%)
  other arithmetic  25.1 us (12%)
    ppermute x8, waiting for transfers between devices, passed_along(): lax.ppermute(value, axis, [(i, (i + by) % devices) for i in range(devices)])  41.8 us
    ppermute x3, starting transfers between devices, from_partner(): lax.ppermute(value, axis, [(i, i ^ 1 << distance) for i in range(lax.axis...  23.2 us
    ppermute x8, starting transfers between devices, passed_along(): lax.ppermute(value, axis, [(i, (i + by) % devices) for i in range(devices)])  16.4 us
    dot_general x4, matrix products, project(): jnp.dot(windows.reshape(-1, windows.shape[-1]), weight, preferred_element...  11.7 us
    convert_element_type x5, local copies, waits for them, and re-layouts, unit_heads(): shaped = tensor_in.reshape(tensor_in.shape[:-1] + (head_count, tensor_in....  9.97 us
    convert_element_type x4, local copies, waits for them, and re-layouts, attend(): return mixture.reshape(queries.shape).astype(jnp.bfloat16)  6.99 us
    dot_general x2, matrix products, attend(): jnp.einsum('nahd,nbhd->nhab', query_unit, key_unit, preferred_element_typ...  6.73 us
    reduce_sum x4, other arithmetic, unit_heads(): jnp.sum(shaped * shaped, axis=-1, keepdims=True) + unit_eps  6.02 us
  transfers between devices with their start and end apart: 11, of which 10 were waited for; matrix products, arithmetic and copies ran while one was open for 3% of the time, Pallas kernels for 0%

commit v1 on v0

v1 whole, which is shorter than its diff:
```python
import functools

import jax
import jax.numpy as jnp
import numpy as np
from jax import lax
from jax.experimental import pallas as pl
from jax.experimental.pallas import tpu as pltpu
from jax.sharding import PartitionSpec as P

ATOM = 40
CELLS = 36
WIN = 4 * ATOM
MESH = pl.DeviceIdType.MESH
BF16 = jnp.bfloat16
F32 = jnp.float32
LOG2E = 1.4426950408889634
NORM_EPS = 1e-05
UNIT_EPS = 1e-06


def level_of(p, j):
    return (2 * p + j + 1) % 4


@functools.lru_cache(None)
def tables():
    cut = np.zeros((160, 192), np.float32)
    for half in range(2):
        for p in range(2):
            for i in range(3):
                for j in range(2):
                    for c in range(6):
                        row = half * 80 + p * 40 + (i * 2 + j) * 6 + c
                        cut[row, (level_of(p, j) * 3 + i) * 16 + half * 6 + c] = 1
    pick = np.zeros((320, 320), np.float32)
    for cp in range(2):
        for rp in range(2):
            for p in range(2):
                for u in range(2):
                    for i in range(3):
                        for j in range(2):
                            for c in range(3):
                                row = (cp * 2 + rp) * 80 + p * 40 + u * 18 + (i * 2 + j) * 3 + c
                                fine = 6 * u + 2 * i + rp
                                col = fine // 3 * 80 + p * 40 + (fine % 3 * 2 + j) * 6 + 2 * c + cp
                                pick[row, col] = 1
    late = np.zeros((256, 160), np.float32)
    early = np.zeros((192, 160), np.float32)
    for half in range(2):
        for j in range(2):
            for u in range(2):
                for i in range(3):
                    for c in range(6):
                        src = (2 * half + c // 3) * 40 + u * 18 + (i * 2 + j) * 3 + c % 3
                        late[(u * 4 + half * 2 + j) * 32 + i * 6 + c, src] = 1
                        early[(half * 2 + j) * 48 + u * 18 + i * 6 + c, src] = 1
    place = np.zeros((192, 224), np.float32)
    for row in range(12):
        for col in range(12):
            half, c = (1, col) if col < 6 else (0, col - 6)
            if row < 3:
                src = 160 + half * 32 + row * 6 + c
            elif row < 9:
                src = half * 48 + (row - 3) * 6 + c
            else:
                src = 96 + half * 32 + (row - 9) * 6 + c
            place[row * 16 + col, src] = 1
    t = np.arange(WIN) % ATOM
    atom = np.arange(WIN) // ATOM
    keep = np.stack(
        [
            (t // 6 % 2)[:, None] == (t // 6 % 2)[None],
            (atom % 2)[:, None] == (atom % 2)[None],
            (t % 18 // 3 % 2)[:, None] == (t % 18 // 3 % 2)[None],
            (t < 18)[:, None] == (t < 18)[None],
        ]
    ).astype(np.float32)
    valid = np.broadcast_to((t < CELLS)[:, None], (WIN, 128)).astype(np.float32)
    group = np.arange(256) // 64
    heads = (group[:, None] == group[None]).astype(np.float32)
    b = lambda x: x.astype(jnp.bfloat16)
    return b(cut), b(pick), b(late), b(early), b(place), b(keep), valid, b(heads)


def layer_norm(values, gain, offset):
    average = jnp.mean(values, axis=-1, keepdims=True)
    centred = values - average
    spread = jnp.mean(centred * centred, axis=-1, keepdims=True)
    return centred * lax.rsqrt(spread + NORM_EPS) * gain + offset


def dot(a, b):
    return jnp.dot(a, b, preferred_element_type=F32)


def project(x, weight_ref, heads_ref, yn):
    for at in range(6):
        lanes = pl.ds(256 * at, 256)
        y = dot(x, weight_ref[:, lanes]).astype(BF16).astype(F32)
        if at < 4:
            y = y * lax.rsqrt(dot((y * y).astype(BF16), heads_ref[...]) + UNIT_EPS)
        yn[:, :, :, lanes] = y.reshape(4, 2, ATOM, 256)


def attend(yn, ctx, w, mask, valid_ref, scale_ref):
    low = lax.broadcasted_iota(jnp.int32, (WIN, 128), 1) < 64
    valid = valid_ref[...]
    zero = jnp.zeros_like(valid)
    for g in range(4):
        q = yn[:, w, :, pl.ds(128 * g, 128)].reshape(WIN, 128).astype(BF16)
        k = yn[:, w, :, pl.ds(512 + 128 * g, 128)].reshape(WIN, 128)
        v = yn[:, w, :, pl.ds(1024 + 128 * g, 128)].reshape(WIN, 128) * valid
        sides = []
        for side in range(2):
            mine = low if side == 0 else jnp.logical_not(low)
            key = jnp.where(mine, k, zero).astype(BF16)
            value = jnp.where(mine, v, valid).astype(BF16)
            score = lax.dot_general(q, key, (((1,), (1,)), ((), ())), preferred_element_type=F32)
            weight = jnp.exp2(score * (scale_ref[2 * g + side] * LOG2E)).astype(BF16) * mask
            sides.append(dot(weight, value))
        top = jnp.where(low, sides[0], sides[1])
        total = pltpu.roll(jnp.where(low, sides[1], sides[0]), 64, 1)
        ctx[:, w, :, pl.ds(128 * g, 128)] = (top / total).reshape(4, ATOM, 128)


def kernel(
    nlat, nlon,
    feat_hbm, packed1_hbm, out1_hbm, merge_hbm, packed2_hbm, out2_hbm,
    scale1, gain1, offset1, gainm, offsetm, scale2, gain2, offset2,
    cut, pick, late, early, place, keep, valid, heads,
    out,
    feat, packed1, wout1, wmerge, packed2, wout2,
    padded, send0, sendr, x, yn, ctx, first, picked, merged, mb, quarter, t0, t1, t2, r0, r1, r2,
    load_sem, s1, v1, s2, v2, s3, v3, s4, v4,
):
    lat, lon = lax.axis_index("lat"), lax.axis_index("lon")
    odd = lax.rem(lon, 2)
    even = odd == 0

    def peer(dlat, dlon):
        return (lax.rem(lat + dlat + nlat, nlat), lax.rem(lon + dlon + nlon, nlon))

    def send(src, dst, send_sem, recv_sem, where):
        return pltpu.make_async_remote_copy(
            src_ref=src, dst_ref=dst, send_sem=send_sem, recv_sem=recv_sem,
            device_id=where, device_id_type=MESH,
        )

    loads = [
        pltpu.make_async_copy(a, b, load_sem.at[n])
        for n, (a, b) in enumerate(
            [(feat_hbm, feat), (packed1_hbm, packed1), (out1_hbm, wout1),
             (merge_hbm, wmerge), (packed2_hbm, packed2), (out2_hbm, wout2)]
        )
    ]
    for load in loads:
        load.start()

    barrier = pltpu.get_barrier_semaphore()
    for dlat, dlon in [
        (0, 1), (0, -1), (0, -2), (1, 0), (1, 1), (-1, 0), (-1, -1), (-1, -2),
        (0, jnp.where(even, 2, -3)), (-1, jnp.where(even, 1, -3)),
    ]:
        pl.semaphore_signal(barrier, inc=1, device_id=peer(dlat, dlon), device_id_type=MESH)

    padded[...] = jnp.zeros_like(padded)
    loads[0].wait()
    for level in range(4):
        padded[level, :, 0:12, :] = feat[level]
    pl.semaphore_wait(barrier, jnp.where(even, 11, 9))

    feature_copies = [
        send(send0.at[pl.ds(2 * n + 1, 2)], x.at[1, pl.ds(2 * n, 2)], s1.at[n], v1.at[n], peer(0, -1))
        for n in range(3)
    ] + [
        send(send0.at[pl.ds(7, 1)], x.at[1, pl.ds(6, 1)], s1.at[3], v1.at[3], peer(0, -1)),
        send(send0.at[pl.ds(0, 1)], x.at[1, pl.ds(7, 1)], s1.at[4], v1.at[4], peer(-1, -1)),
        send(sendr, x.at[0, pl.ds(7, 1)], s1.at[5], v1.at[5], peer(-1, 0)),
    ]
    for n, hb in enumerate([1, 2, 3, 4, 5, 6, 7, 0]):
        tokens = padded[:, pl.ds(3 * hb, 3)].reshape(192, 512)
        atoms = dot(cut[...], tokens).astype(BF16)
        send0[hb] = atoms[:80]
        if hb > 0:
            x[0, hb - 1] = atoms[80:]
        else:
            sendr[0] = atoms[80:]
        if n in (1, 3, 5):
            feature_copies[n // 2].start()
        if n == 6:
            feature_copies[3].start()
    feature_copies[4].start()
    feature_copies[5].start()

    loads[1].wait()
    loads[2].wait()
    edge = send(first.at[:, pl.ds(0, 1)], first.at[:, pl.ds(8, 1)], s2, v2, peer(-1, 0))
    last_lat = lat == nlat - 1

    def band(b, carry):
        for n in range(3):
            @pl.when(b == n)
            def _():
                feature_copies[n].wait_recv()

        @pl.when(b == 3)
        def _():
            for n in range(3, 6):
                feature_copies[n].wait_recv()

        xb = x[:, pl.ds(2 * b, 2)].reshape(320, 512)
        project(xb, packed1, heads, yn)
        wrapped = jnp.where(jnp.logical_and(last_lat, b == 3), 1.0, 0.0).astype(F32)
        rows = keep[1].astype(F32) * wrapped + (1.0 - wrapped)
        attend(yn, ctx, 0, rows.astype(BF16), valid, scale1)
        attend(yn, ctx, 1, (rows * keep[0].astype(F32)).astype(BF16), valid, scale1)
        branch = layer_norm(
            dot(ctx[...].reshape(320, 512).astype(BF16), wout1[...]), gain1[...], offset1[...]
        )
        first[:, pl.ds(2 * b, 2)] = (xb.astype(F32) + branch).astype(BF16).reshape(2, 2, 80, 512)

        @pl.when(b == 0)
        def _():
            edge.start()
        return carry

    lax.fori_loop(0, 4, band, 0)

    edge.wait_recv()
    for half in range(2):
        for cb in range(2):
            fine = first[half, pl.ds(4 * cb + 1, 4)].reshape(320, 512)
            parts = dot(pick[...], fine).astype(BF16)
            for at in range(4):
                picked[pl.ds((half * 2 + cb) * 80, 80), pl.ds(512 * at, 512)] = parts[80 * at : 80 * at + 80]
    loads[3].wait()
    normed = layer_norm(dot(picked[...], wmerge[...]), gainm[...], offsetm[...])
    merged[...] = normed.reshape(2, 2, 2, ATOM, 1024)
    for half in range(2):
        for p in range(2):
            mb[half, p] = merged[half, :, p].reshape(80, 1024).astype(BF16)
    even_copies = [
        send(mb.at[0, 0], quarter.at[3], s3.at[0], v3.at[3], peer(0, -2)),
        send(mb.at[0, 1], quarter.at[3], s3.at[1], v3.at[3], peer(0, -1)),
        send(mb.at[1, 1], quarter.at[0], s3.at[2], v3.at[0], peer(0, 1)),
    ]
    odd_copies = [
        send(mb.at[0, 0], quarter.at[1], s3.at[0], v3.at[1], peer(0, -1)),
        send(mb.at[1, 0], quarter.at[2], s3.at[1], v3.at[2], peer(0, -1)),
    ]

    @pl.when(even)
    def _():
        for copy in even_copies:
            copy.start()
        quarter[0] = mb[1, 0]
        odd_copies[0].wait_recv()
        odd_copies[1].wait_recv()
        even_copies[0].wait_recv()

    @pl.when(jnp.logical_not(even))
    def _():
        for copy in odd_copies:
            copy.start()
        quarter[1] = mb[0, 1]
        quarter[2] = mb[1, 1]
        even_copies[2].wait_recv()
        even_copies[0].wait_recv()

    loads[4].wait()
    loads[5].wait()
    tokens = quarter[...]
    project(tokens.reshape(320, 1024), packed2, heads, yn)
    upper = odd.astype(F32)
    levels = keep[2].astype(F32) * upper + (1.0 - upper)
    final_copies = []
    for cb in (1, 0):
        if cb == 1:
            wrapped = jnp.where(last_lat, 1.0, 0.0).astype(F32)
            mask = levels * (keep[3].astype(F32) * wrapped + (1.0 - wrapped))
        else:
            mask = levels
        attend(yn, ctx, cb, mask.astype(BF16), valid, scale2)
        branch = layer_norm(
            dot(ctx[:, cb].reshape(WIN, 512).astype(BF16), wout2[...]), gain2[...], offset2[...]
        )
        own = quarter[...].astype(F32)[:, 40 * cb : 40 * cb + 40].reshape(WIN, 1024)
        second = (own + branch).astype(BF16)
        if cb == 1:
            units = dot(late[...], second).astype(BF16).reshape(2, 2, 2, 32, 1024)
            r1[0, 0] = units[0, 0, 0]
            t1[...] = units[0]
            t2[...] = units[1]
        else:
            units = dot(early[...], second).astype(BF16).reshape(2, 2, 48, 1024)
            r0[0, 0] = units[0, 0]
            t0[...] = units
        for half in range(2):
            for j in range(2):
                to = 2 * half + (0 if j == 0 else 1 - 2 * odd)
                n = half * 2 + j
                if cb == 1:
                    final_copies.append(
                        send(t2.at[half, j], r2.at[half, j], s4.at[n], v4.at[n], peer(1, to)))
                    final_copies[-1].start()
                if n > 0:
                    src, dst, base = (t1, r1, 3) if cb == 1 else (t0, r0, 6)
                    final_copies.append(
                        send(src.at[half, j], dst.at[half, j], s4.at[base + n], v4.at[base + n], peer(0, to)))
                    final_copies[-1].start()

    for copy in final_copies:
        copy.wait_recv()
    for level in range(2):
        j = 1 - level
        parts = [r[half, j] for r in (r0, r1, r2) for half in range(2)]
        rows = dot(place[...], jnp.concatenate(parts, axis=0))
        out[:, 0, level] = rows.astype(BF16).reshape(12, 16, 1024)[:, :12]

    for copy in feature_copies:
        copy.wait_send()
    edge.wait_send()

    @pl.when(even)
    def _():
        for copy in even_copies:
            copy.wait_send()

    @pl.when(jnp.logical_not(even))
    def _():
        for copy in odd_copies:
            copy.wait_send()

    for copy in final_copies:
        copy.wait_send()


def body(nlat, nlon, features, packed_first, scale_first, output_first, gain_first, offset_first,
         merge_weight, merge_gain, merge_offset,
         packed_second, scale_second, output_second, gain_second, offset_second):
    any_spec = pl.BlockSpec(memory_space=pl.ANY)
    vmem = pl.BlockSpec(memory_space=pltpu.VMEM)
    smem = pl.BlockSpec(memory_space=pltpu.SMEM)
    dma = pltpu.SemaphoreType.DMA
    row = lambda v: v.reshape(1, -1)
    return pl.pallas_call(
        functools.partial(kernel, nlat, nlon),
        out_shape=jax.ShapeDtypeStruct((12, 1, 2, 12, 1024), BF16),
        in_specs=[any_spec] * 6 + [smem] + [vmem] * 4 + [smem] + [vmem] * 2 + [vmem] * 8,
        out_specs=vmem,
        scratch_shapes=[
            pltpu.VMEM((4, 24, 12, 512), BF16),
            pltpu.VMEM((512, 1536), BF16),
            pltpu.VMEM((512, 512), BF16),
            pltpu.VMEM((2048, 1024), BF16),
            pltpu.VMEM((1024, 1536), BF16),
            pltpu.VMEM((512, 1024), BF16),
            pltpu.VMEM((4, 24, 16, 512), BF16),
            pltpu.VMEM((8, 80, 512), BF16),
            pltpu.VMEM((1, 80, 512), BF16),
            pltpu.VMEM((2, 8, 80, 512), BF16),
            pltpu.VMEM((4, 2, ATOM, 1536), F32),
            pltpu.VMEM((4, 2, ATOM, 512), F32),
            pltpu.VMEM((2, 9, 80, 512), BF16),
            pltpu.VMEM((320, 2048), BF16),
            pltpu.VMEM((2, 2, 2, ATOM, 1024), F32),
            pltpu.VMEM((2, 2, 80, 1024), BF16),
            pltpu.VMEM((4, 80, 1024), BF16),
            pltpu.VMEM((2, 2, 48, 1024), BF16),
            pltpu.VMEM((2, 2, 32, 1024), BF16),
            pltpu.VMEM((2, 2, 32, 1024), BF16),
            pltpu.VMEM((2, 2, 48, 1024), BF16),
            pltpu.VMEM((2, 2, 32, 1024), BF16),
            pltpu.VMEM((2, 2, 32, 1024), BF16),
            dma((6,)),
            dma((6,)), dma((6,)),
            dma, dma,
            dma((3,)), dma((4,)),
            dma((10,)), dma((10,)),
        ],
        compiler_params=pltpu.CompilerParams(
            collective_id=0, has_side_effects=True, vmem_limit_bytes=52 * 2**20
        ),
        cost_estimate=pl.CostEstimate(flops=6_000_000_000, bytes_accessed=14_000_000, transcendentals=2_000_000),
    )(
        features, packed_first, output_first, merge_weight, packed_second, output_second,
        scale_first, row(gain_first), row(offset_first), row(merge_gain), row(merge_offset),
        scale_second, row(gain_second), row(offset_second),
        *[jnp.asarray(t) for t in tables()],
    )


def solution(mesh):
    return jax.shard_map(
        functools.partial(body, mesh.shape["lat"], mesh.shape["lon"]),
        mesh=mesh,
        in_specs=(P(None, "lat", "lon", None),) + (P(),) * 13,
        out_specs=P("lat", "lon", None, None, None),
        check_vma=False,
    )
```

time: 204 us -> 56.7 us (0.28); the launches traced: 200 us -> 56.6 us
  local copies, waits for them, and re-layouts: 62.1 us -> 5.66 us
  Pallas kernels: 0 us -> 50.7 us
  waiting for transfers between devices: 44.2 us -> 0 us
  starting transfers between devices: 39.7 us -> 0 us
  matrix products: 28 us -> 0 us
  other arithmetic: 25.1 us -> 0 us
    pallas_call x0 -> x1, Pallas kernels: none -> 50.7 us  [body(): pl.pallas_call(functools.partial(kernel, nlat, nlon), out_shape=jax.Shape...]
    ppermute x11 -> x0, waiting for transfers between devices: 44.2 us -> none  [the longest x8 41.8 us: passed_along(): lax.ppermute(value, axis, [(i, (i + by) % devices) for i in range(devices)])]
    ppermute x11 -> x0, starting transfers between devices: 39.7 us -> none  [the longest x3 23.2 us: from_partner(): lax.ppermute(value, axis, [(i, i ^ 1 << distance) for i in range(lax.axis...]
    dot_general x12 -> x0, matrix products: 28 us -> none  [the longest x4 11.7 us: project(): jnp.dot(windows.reshape(-1, windows.shape[-1]), weight, preferred_element...]
    convert_element_type x9 -> x0, local copies, waits for them, and re-layouts: 17 us -> none  [the longest x5 9.97 us: unit_heads(): shaped = tensor_in.reshape(tensor_in.shape[:-1] + (head_count, tensor_in....]
    reshape x8 -> x0, local copies, waits for them, and re-layouts: 14.3 us -> none  [the longest x1 3.32 us: from_windows(): return shaped.reshape(levels, row_count, col_count * width)]
    convert_element_type x8 -> x0, other arithmetic: 9.59 us -> none  [the longest x1 4.12 us: finish(): return (residual.astype(jnp.float32) + branch).astype(jnp.bfloat16)]
    slice x11 -> x0, local copies, waits for them, and re-layouts: 9.49 us -> none  [the longest x1 3.75 us: body(): pairs[..., inner_width:]]
  transfers between devices with their start and end apart: 11 -> 0, of which waited for: 10 -> 0; matrix products, arithmetic and copies ran while one was open for 3% -> 0% of each run, Pallas kernels for 0% -> 0%
where the time goes in v1:
time: 56.7 us; the launch traced here: 56.6 us
  Pallas kernels  50.7 us (89%)
  local copies, waits for them, and re-layouts  5.66 us (10%)
    pallas_call x1, Pallas kernels, body(): pl.pallas_call(functools.partial(kernel, nlat, nlon), out_shape=jax.Shape...  50.7 us
    unnamed x35, local copies, waits for them, and re-layouts  3.11 us
    pallas_call x1, local copies, waits for them, and re-layouts, body(): pl.pallas_call(functools.partial(kernel, nlat, nlon), out_shape=jax.Shape...  2.56 us

profile of v1, /device:TPU:1, one launch (start us, length us, event | category | flops | bytes accessed | tf_op | source)
XLA Modules:
  0.0 56.6 jit_solution(4433165005115109155)
XLA Ops:
  0.0 0.0 copy-start.11
  0.0 0.0 copy-start.15
  0.0 0.0 copy-start.9
  0.0 0.0 copy-start.13
  0.0 0.0 copy-start.14
  0.0 0.0 copy-start.12
  0.0 0.0 copy-start.10
  0.1 0.0 copy-start.16
  0.1 0.0 copy-start.4
  0.1 0.0 copy-start.3
  0.1 0.0 copy-start.8
  0.1 0.0 copy-start.2
  0.1 0.0 copy-start.1
  0.1 0.0 copy-start.6
  0.1 0.0 copy-start.5
  0.1 0.0 copy-start
  0.2 0.0 copy-start.7
  0.2 3.0 %copy.23.feat_hbm = bf16[4,24,12,512]{3,2,1,0:T(8,128)(2,1)} copy(bf16[4,24,12,512]{3,1,2,0:T(8,128)(2,1)} %param.22) | data formatting | bytes 2359296 | tf_op args[0]
  3.2 0.0 copy-done.11
  3.2 0.0 copy-done.15
  3.2 0.0 copy-done.9
  3.2 0.0 copy-done.13
  3.2 0.0 copy-done.14
  3.2 0.0 copy-done.12
  3.2 0.0 copy-done.10
  3.2 0.0 copy-done.16
  3.2 0.0 copy-done.4
  3.3 0.0 copy-done.3
  3.3 0.0 copy-done.8
  3.3 0.0 copy-done.2
  3.3 0.0 copy-done.1
  3.3 0.0 copy-done.6
  3.3 0.0 copy-done.5
  3.3 0.0 copy-done
  3.3 0.0 copy-done.7
  3.3 50.7 %shard_map.208 = bf16[12,1,2,12,1024]{4,3,2,1,0:T(8,128)(2,1)} custom-call(bf16[4,24,12,512]{3,2,1,0:T(8,128)(2,1)} %copy.23.feat_hbm, bf16[512,1536]{1,0:T(8,128)(2,1)} %packed1_hbm.1, bf16[512,512]{1,0:T(8,128)(2,1)S(1)} %copy-done, bf16[2048,1024]{1,0:T(8,128)(2,1)} %merge_hbm.1, bf16[1024,1536]{1,0:T(8,128)(2,1)} %packed2_hbm.1, ...), custom_call_target="tpu_custom_call" | custom-call | flops 6000000000 | bytes 14000000 | tf_op jit(solution)/shard_map/pallas_call | solution.py:347
  54.0 2.6 %copy.24 = bf16[12,1,2,12,1024]{4,2,3,1,0:T(2,128)(2,1)} copy(bf16[12,1,2,12,1024]{4,3,2,1,0:T(8,128)(2,1)} %shard_map.208) | data formatting | bytes 1179648 | tf_op jit(solution)/shard_map/pallas_call | solution.py:347
Async XLA Ops:
  0.0 3.2 %copy-start.11 = (bf16[256,256]{1,0:T(8,128)(2,1)S(1)}, bf16[256,256]{1,0:T(8,128)(2,1)}, u32[]{:S(2)}) copy-start(bf16[256,256]{1,0:T(8,128)(2,1)} %constant.23.clone.heads) | copy-start | bytes 393220
  0.0 3.2 %copy-start.15 = (f32[160,128]{1,0:T(8,128)S(1)}, f32[160,128]{1,0:T(8,128)}, u32[]{:S(2)}) copy-start(f32[160,128]{1,0:T(8,128)} %constant.22.clone.valid) | copy-start | bytes 245764
  0.0 3.2 %copy-start.9 = (bf16[4,160,160]{2,1,0:T(8,128)(2,1)S(1)}, bf16[4,160,160]{2,1,0:T(8,128)(2,1)}, u32[]{:S(2)}) copy-start(bf16[4,160,160]{2,1,0:T(8,128)(2,1)} %constant.21.clone.keep) | copy-start | bytes 614404
  0.0 3.2 %copy-start.13 = (bf16[192,224]{1,0:T(8,128)(2,1)S(1)}, bf16[192,224]{1,0:T(8,128)(2,1)}, u32[]{:S(2)}) copy-start(bf16[192,224]{1,0:T(8,128)(2,1)} %constant.20.clone.place) | copy-start | bytes 258052
  0.0 3.2 %copy-start.14 = (bf16[192,160]{1,0:T(8,128)(2,1)S(1)}, bf16[192,160]{1,0:T(8,128)(2,1)}, u32[]{:S(2)}) copy-start(bf16[192,160]{1,0:T(8,128)(2,1)} %constant.19.clone.early) | copy-start | bytes 184324
  0.0 3.2 %copy-start.12 = (bf16[256,160]{1,0:T(8,128)(2,1)S(1)}, bf16[256,160]{1,0:T(8,128)(2,1)}, u32[]{:S(2)}) copy-start(bf16[256,160]{1,0:T(8,128)(2,1)} %constant.18.clone.late) | copy-start | bytes 245764
  0.0 3.2 %copy-start.10 = (bf16[320,320]{1,0:T(8,128)(2,1)S(1)}, bf16[320,320]{1,0:T(8,128)(2,1)}, u32[]{:S(2)}) copy-start(bf16[320,320]{1,0:T(8,128)(2,1)} %constant.17.clone.pick) | copy-start | bytes 614404
  0.1 3.2 %copy-start.16 = (bf16[160,192]{1,0:T(8,128)(2,1)S(1)}, bf16[160,192]{1,0:T(8,128)(2,1)}, u32[]{:S(2)}) copy-start(bf16[160,192]{1,0:T(8,128)(2,1)} %constant.16.clone.cut) | copy-start | bytes 184324
  0.1 3.2 %copy-start.4 = (f32[1024]{0:T(1024)S(1)}, f32[1024]{0:T(1024)}, u32[]{:S(2)}) copy-start(f32[1024]{0:T(1024)} %param.35) | copy-start | bytes 12292
  0.1 3.2 %copy-start.3 = (f32[1024]{0:T(1024)S(1)}, f32[1024]{0:T(1024)}, u32[]{:S(2)}) copy-start(f32[1024]{0:T(1024)} %param.34) | copy-start | bytes 12292
  0.1 3.2 %copy-start.8 = (f32[8]{0:T(128)S(1)}, f32[8]{0:T(128)}, u32[]{:S(2)}) copy-start(f32[8]{0:T(128)} %scale2.1) | copy-start | bytes 100
  0.1 3.2 %copy-start.2 = (f32[1024]{0:T(1024)S(1)}, f32[1024]{0:T(1024)}, u32[]{:S(2)}) copy-start(f32[1024]{0:T(1024)} %param.30) | copy-start | bytes 12292
  0.1 3.2 %copy-start.1 = (f32[1024]{0:T(1024)S(1)}, f32[1024]{0:T(1024)}, u32[]{:S(2)}) copy-start(f32[1024]{0:T(1024)} %param.29) | copy-start | bytes 12292
  0.1 3.2 %copy-start.6 = (f32[512]{0:T(512)S(1)}, f32[512]{0:T(512)}, u32[]{:S(2)}) copy-start(f32[512]{0:T(512)} %param.27) | copy-start | bytes 6148
  0.1 3.2 %copy-start.5 = (f32[512]{0:T(512)S(1)}, f32[512]{0:T(512)}, u32[]{:S(2)}) copy-start(f32[512]{0:T(512)} %param.26) | copy-start | bytes 6148
  0.1 3.2 %copy-start = (bf16[512,512]{1,0:T(8,128)(2,1)S(1)}, bf16[512,512]{1,0:T(8,128)(2,1)}, u32[]{:S(2)}) copy-start(bf16[512,512]{1,0:T(8,128)(2,1)} %out1_hbm.1) | copy-start | bytes 1572868
  0.2 3.2 %copy-start.7 = (f32[8]{0:T(128)S(1)}, f32[8]{0:T(128)}, u32[]{:S(2)}) copy-start(f32[8]{0:T(128)} %scale1.1) | copy-start | bytes 100

commit v2 on v1

--- a/solution.py
+++ b/solution.py
@@ -25,14 +25,14 @@
 
 @functools.lru_cache(None)
 def tables():
-    cut = np.zeros((160, 192), np.float32)
-    for half in range(2):
-        for p in range(2):
+    cut = np.zeros((2, 160, 192), np.float32)
+    for part in range(2):
+        for hb in range(4):
             for i in range(3):
                 for j in range(2):
                     for c in range(6):
-                        row = half * 80 + p * 40 + (i * 2 + j) * 6 + c
-                        cut[row, (level_of(p, j) * 3 + i) * 16 + half * 6 + c] = 1
+                        row = hb * 40 + (i * 2 + j) * 6 + c
+                        cut[part, row, (j * 6 + c) * 16 + 3 * hb + i + 4 * part] = 1
     pick = np.zeros((320, 320), np.float32)
     for cp in range(2):
         for rp in range(2):
@@ -45,27 +45,29 @@
                                 fine = 6 * u + 2 * i + rp
                                 col = fine // 3 * 80 + p * 40 + (fine % 3 * 2 + j) * 6 + 2 * c + cp
                                 pick[row, col] = 1
-    late = np.zeros((256, 160), np.float32)
-    early = np.zeros((192, 160), np.float32)
+    late = np.zeros((640, 640), np.float32)
+    early = np.zeros((576, 640), np.float32)
     for half in range(2):
         for j in range(2):
             for u in range(2):
                 for i in range(3):
                     for c in range(6):
                         src = (2 * half + c // 3) * 40 + u * 18 + (i * 2 + j) * 3 + c % 3
-                        late[(u * 4 + half * 2 + j) * 32 + i * 6 + c, src] = 1
-                        early[(half * 2 + j) * 48 + u * 18 + i * 6 + c, src] = 1
-    place = np.zeros((192, 224), np.float32)
-    for row in range(12):
-        for col in range(12):
-            half, c = (1, col) if col < 6 else (0, col - 6)
-            if row < 3:
-                src = 160 + half * 32 + row * 6 + c
-            elif row < 9:
-                src = half * 48 + (row - 3) * 6 + c
-            else:
-                src = 96 + half * 32 + (row - 9) * 6 + c
-            place[row * 16 + col, src] = 1
+                        for lane in range(4):
+                            late[(u * 4 + half * 2 + j) * 80 + lane * 18 + i * 6 + c, lane * 160 + src] = 1
+                            early[(half * 2 + j) * 144 + lane * 36 + u * 18 + i * 6 + c, lane * 160 + src] = 1
+    place = np.zeros((4, 144, 608), np.float32)
+    for lane in range(4):
+        for row in range(12):
+            for col in range(12):
+                half, c = (1, col) if col < 6 else (0, col - 6)
+                if row < 3:
+                    src = 448 + 80 * half + lane * 18 + row * 6 + c
+                elif row < 9:
+                    src = 144 * half + lane * 36 + (row - 3) * 6 + c
+                else:
+                    src = 288 + 80 * half + lane * 18 + (row - 9) * 6 + c
+                place[lane, row * 12 + col, src] = 1
     t = np.arange(WIN) % ATOM
     atom = np.arange(WIN) // ATOM
     keep = np.stack(
@@ -94,13 +96,13 @@
     return jnp.dot(a, b, preferred_element_type=F32)
 
 
-def project(x, weight_ref, heads_ref, yn):
+def project(x, weight_ref, heads_ref, yn, start, count):
     for at in range(6):
         lanes = pl.ds(256 * at, 256)
         y = dot(x, weight_ref[:, lanes]).astype(BF16).astype(F32)
         if at < 4:
             y = y * lax.rsqrt(dot((y * y).astype(BF16), heads_ref[...]) + UNIT_EPS)
-        yn[:, :, :, lanes] = y.reshape(4, 2, ATOM, 256)
+        yn[pl.ds(start, count), :, :, lanes] = y.reshape(count, 2, ATOM, 256)
 
 
 def attend(yn, ctx, w, mask, valid_ref, scale_ref):
@@ -127,11 +129,12 @@
 def kernel(
     nlat, nlon,
     feat_hbm, packed1_hbm, out1_hbm, merge_hbm, packed2_hbm, out2_hbm,
+    pick_hbm, late_hbm, early_hbm, place_hbm,
     scale1, gain1, offset1, gainm, offsetm, scale2, gain2, offset2,
-    cut, pick, late, early, place, keep, valid, heads,
+    cut, keep, valid, heads,
     out,
-    feat, packed1, wout1, wmerge, packed2, wout2,
-    padded, send0, sendr, x, yn, ctx, first, picked, merged, mb, quarter, t0, t1, t2, r0, r1, r2,
+    feat, packed1, wout1, wmerge, packed2, wout2, pick, late, early, place,
+    send0, sendr, x, yn, ctx, first, picked, mb, quarter, t0, t1, t2, r0, r1, r2,
     load_sem, s1, v1, s2, v2, s3, v3, s4, v4,
 ):
     lat, lon = lax.axis_index("lat"), lax.axis_index("lon")
@@ -151,7 +154,8 @@
         pltpu.make_async_copy(a, b, load_sem.at[n])
         for n, (a, b) in enumerate(
             [(feat_hbm, feat), (packed1_hbm, packed1), (out1_hbm, wout1),
-             (merge_hbm, wmerge), (packed2_hbm, packed2), (out2_hbm, wout2)]
+             (merge_hbm, wmerge), (packed2_hbm, packed2), (out2_hbm, wout2),
+             (pick_hbm, pick), (late_hbm, late), (early_hbm, early), (place_hbm, place)]
         )
     ]
     for load in loads:
@@ -164,10 +168,7 @@
     ]:
         pl.semaphore_signal(barrier, inc=1, device_id=peer(dlat, dlon), device_id_type=MESH)
 
-    padded[...] = jnp.zeros_like(padded)
     loads[0].wait()
-    for level in range(4):
-        padded[level, :, 0:12, :] = feat[level]
     pl.semaphore_wait(barrier, jnp.where(even, 11, 9))
 
     feature_copies = [
@@ -178,20 +179,29 @@
         send(send0.at[pl.ds(0, 1)], x.at[1, pl.ds(7, 1)], s1.at[4], v1.at[4], peer(-1, -1)),
         send(sendr, x.at[0, pl.ds(7, 1)], s1.at[5], v1.at[5], peer(-1, 0)),
     ]
-    for n, hb in enumerate([1, 2, 3, 4, 5, 6, 7, 0]):
-        tokens = padded[:, pl.ds(3 * hb, 3)].reshape(192, 512)
-        atoms = dot(cut[...], tokens).astype(BF16)
-        send0[hb] = atoms[:80]
-        if hb > 0:
-            x[0, hb - 1] = atoms[80:]
-        else:
-            sendr[0] = atoms[80:]
-        if n in (1, 3, 5):
-            feature_copies[n // 2].start()
-        if n == 6:
-            feature_copies[3].start()
-    feature_copies[4].start()
-    feature_copies[5].start()
+    for half in range(2):
+        for part in range(2):
+            pair = []
+            for p in range(2):
+                tokens = jnp.stack([
+                    feat[level_of(p, j), 6 * half : 6 * half + 6].astype(F32)[:, 8 * part : 8 * part + 16]
+                    for j in range(2)
+                ]).astype(BF16).reshape(192, 512)
+                pair.append(dot(cut[part], tokens).reshape(4, ATOM, 512))
+            atoms = jnp.concatenate(pair, axis=1).astype(BF16)
+            if half == 0:
+                send0[pl.ds(4 * part, 4)] = atoms
+                if part == 0:
+                    feature_copies[0].start()
+                else:
+                    for copy in feature_copies[1:5]:
+                        copy.start()
+            elif part == 0:
+                sendr[...] = atoms[:1]
+                feature_copies[5].start()
+                x[0, pl.ds(0, 3)] = atoms[1:]
+            else:
+                x[0, pl.ds(3, 4)] = atoms
 
     loads[1].wait()
     loads[2].wait()
@@ -210,7 +220,7 @@
                 feature_copies[n].wait_recv()
 
         xb = x[:, pl.ds(2 * b, 2)].reshape(320, 512)
-        project(xb, packed1, heads, yn)
+        project(xb, packed1, heads, yn, 0, 4)
         wrapped = jnp.where(jnp.logical_and(last_lat, b == 3), 1.0, 0.0).astype(F32)
         rows = keep[1].astype(F32) * wrapped + (1.0 - wrapped)
         attend(yn, ctx, 0, rows.astype(BF16), valid, scale1)
@@ -227,19 +237,6 @@
 
     lax.fori_loop(0, 4, band, 0)
 
-    edge.wait_recv()
-    for half in range(2):
-        for cb in range(2):
-            fine = first[half, pl.ds(4 * cb + 1, 4)].reshape(320, 512)
-            parts = dot(pick[...], fine).astype(BF16)
-            for at in range(4):
-                picked[pl.ds((half * 2 + cb) * 80, 80), pl.ds(512 * at, 512)] = parts[80 * at : 80 * at + 80]
-    loads[3].wait()
-    normed = layer_norm(dot(picked[...], wmerge[...]), gainm[...], offsetm[...])
-    merged[...] = normed.reshape(2, 2, 2, ATOM, 1024)
-    for half in range(2):
-        for p in range(2):
-            mb[half, p] = merged[half, :, p].reshape(80, 1024).astype(BF16)
     even_copies = [
         send(mb.at[0, 0], quarter.at[3], s3.at[0], v3.at[3], peer(0, -2)),
         send(mb.at[0, 1], quarter.at[3], s3.at[1], v3.at[3], peer(0, -1)),
@@ -249,29 +246,45 @@
         send(mb.at[0, 0], quarter.at[1], s3.at[0], v3.at[1], peer(0, -1)),
         send(mb.at[1, 0], quarter.at[2], s3.at[1], v3.at[2], peer(0, -1)),
     ]
-
-    @pl.when(even)
-    def _():
-        for copy in even_copies:
-            copy.start()
-        quarter[0] = mb[1, 0]
-        odd_copies[0].wait_recv()
-        odd_copies[1].wait_recv()
-        even_copies[0].wait_recv()
-
-    @pl.when(jnp.logical_not(even))
-    def _():
-        for copy in odd_copies:
-            copy.start()
-        quarter[1] = mb[0, 1]
-        quarter[2] = mb[1, 1]
-        even_copies[2].wait_recv()
-        even_copies[0].wait_recv()
+    edge.wait_recv()
+    loads[6].wait()
+    loads[3].wait()
+    for half in range(2):
+        for cb in range(2):
+            fine = first[half, pl.ds(4 * cb + 1, 4)].reshape(320, 512)
+            parts = dot(pick[...], fine).astype(BF16)
+            for at in range(4):
+                picked[half, pl.ds(cb * 80, 80), pl.ds(512 * at, 512)] = parts[80 * at : 80 * at + 80]
+        normed = layer_norm(dot(picked[half], wmerge[...]), gainm[...], offsetm[...])
+        pairs = normed.reshape(2, 2, ATOM, 1024)
+        for p in range(2):
+            mb[half, p] = pairs[:, p].reshape(80, 1024).astype(BF16)
+
+        @pl.when(even)
+        def _():
+            if half == 0:
+                even_copies[0].start()
+                even_copies[1].start()
+            else:
+                even_copies[2].start()
+                quarter[0] = mb[1, 0]
+                odd_copies[0].wait_recv()
+                odd_copies[1].wait_recv()
+
+        @pl.when(jnp.logical_not(even))
+        def _():
+            odd_copies[half].start()
+            quarter[1 + half] = mb[half, 1]
+            if half == 1:
+                even_copies[2].wait_recv()
 
     loads[4].wait()
     loads[5].wait()
-    tokens = quarter[...]
-    project(tokens.reshape(320, 1024), packed2, heads, yn)
+    project(quarter[pl.ds(0, 3)].reshape(240, 1024), packed2, heads, yn, 0, 3)
+    even_copies[0].wait_recv()
+    project(quarter[3], packed2, heads, yn, 3, 1)
+    for load in loads[7:]:
+        load.wait()
     upper = odd.astype(F32)
     levels = keep[2].astype(F32) * upper + (1.0 - upper)
     final_copies = []
@@ -287,13 +300,14 @@
         )
         own = quarter[...].astype(F32)[:, 40 * cb : 40 * cb + 40].reshape(WIN, 1024)
         second = (own + branch).astype(BF16)
+        stacked = jnp.concatenate([second[:, 256 * n : 256 * n + 256] for n in range(4)], axis=0)
         if cb == 1:
-            units = dot(late[...], second).astype(BF16).reshape(2, 2, 2, 32, 1024)
+            units = dot(late[...], stacked).astype(BF16).reshape(2, 2, 2, 80, 256)
             r1[0, 0] = units[0, 0, 0]
             t1[...] = units[0]
             t2[...] = units[1]
         else:
-            units = dot(early[...], second).astype(BF16).reshape(2, 2, 48, 1024)
+            units = dot(early[...], stacked).astype(BF16).reshape(2, 2, 144, 256)
             r0[0, 0] = units[0, 0]
             t0[...] = units
         for half in range(2):
@@ -315,8 +329,9 @@
     for level in range(2):
         j = 1 - level
         parts = [r[half, j] for r in (r0, r1, r2) for half in range(2)]
-        rows = dot(place[...], jnp.concatenate(parts, axis=0))
-        out[:, 0, level] = rows.astype(BF16).reshape(12, 16, 1024)[:, :12]
+        parts = jnp.concatenate(parts, axis=0)
+        for n in range(4):
+            out[level, :, pl.ds(256 * n, 256)] = dot(place[n], parts).astype(BF16)
 
     for copy in feature_copies:
         copy.wait_send()
@@ -344,36 +359,40 @@
     smem = pl.BlockSpec(memory_space=pltpu.SMEM)
     dma = pltpu.SemaphoreType.DMA
     row = lambda v: v.reshape(1, -1)
-    return pl.pallas_call(
+    *small, keep, valid, heads = [jnp.asarray(t) for t in tables()]
+    cut, pick, late, early, place = small
+    out = pl.pallas_call(
         functools.partial(kernel, nlat, nlon),
-        out_shape=jax.ShapeDtypeStruct((12, 1, 2, 12, 1024), BF16),
-        in_specs=[any_spec] * 6 + [smem] + [vmem] * 4 + [smem] + [vmem] * 2 + [vmem] * 8,
+        out_shape=jax.ShapeDtypeStruct((2, 144, 1024), BF16),
+        in_specs=[any_spec] * 10 + [smem] + [vmem] * 4 + [smem] + [vmem] * 2 + [vmem] * 4,
         out_specs=vmem,
         scratch_shapes=[
-            pltpu.VMEM((4, 24, 12, 512), BF16),
+            pltpu.VMEM((4, 12, 24, 512), BF16),
             pltpu.VMEM((512, 1536), BF16),
             pltpu.VMEM((512, 512), BF16),
             pltpu.VMEM((2048, 1024), BF16),
             pltpu.VMEM((1024, 1536), BF16),
             pltpu.VMEM((512, 1024), BF16),
-            pltpu.VMEM((4, 24, 16, 512), BF16),
+            pltpu.VMEM((320, 320), BF16),
+            pltpu.VMEM((640, 640), BF16),
+            pltpu.VMEM((576, 640), BF16),
+            pltpu.VMEM((4, 144, 608), BF16),
             pltpu.VMEM((8, 80, 512), BF16),
             pltpu.VMEM((1, 80, 512), BF16),
             pltpu.VMEM((2, 8, 80, 512), BF16),
             pltpu.VMEM((4, 2, ATOM, 1536), F32),
             pltpu.VMEM((4, 2, ATOM, 512), F32),
             pltpu.VMEM((2, 9, 80, 512), BF16),
-            pltpu.VMEM((320, 2048), BF16),
-            pltpu.VMEM((2, 2, 2, ATOM, 1024), F32),
+            pltpu.VMEM((2, 160, 2048), BF16),
             pltpu.VMEM((2, 2, 80, 1024), BF16),
             pltpu.VMEM((4, 80, 1024), BF16),
-            pltpu.VMEM((2, 2, 48, 1024), BF16),
-            pltpu.VMEM((2, 2, 32, 1024), BF16),
-            pltpu.VMEM((2, 2, 32, 1024), BF16),
-            pltpu.VMEM((2, 2, 48, 1024), BF16),
-            pltpu.VMEM((2, 2, 32, 1024), BF16),
-            pltpu.VMEM((2, 2, 32, 1024), BF16),
-            dma((6,)),
+            pltpu.VMEM((2, 2, 144, 256), BF16),
+            pltpu.VMEM((2, 2, 80, 256), BF16),
+            pltpu.VMEM((2, 2, 80, 256), BF16),
+            pltpu.VMEM((2, 2, 144, 256), BF16),
+            pltpu.VMEM((2, 2, 80, 256), BF16),
+            pltpu.VMEM((2, 2, 80, 256), BF16),
+            dma((10,)),
             dma((6,)), dma((6,)),
             dma, dma,
             dma((3,)), dma((4,)),
@@ -384,11 +403,13 @@
         ),
         cost_estimate=pl.CostEstimate(flops=6_000_000_000, bytes_accessed=14_000_000, transcendentals=2_000_000),
     )(
-        features, packed_first, output_first, merge_weight, packed_second, output_second,
+        jnp.transpose(features, (0, 2, 1, 3)), packed_first, output_first, merge_weight, packed_second, output_second,
+        pick, late, early, place,
         scale_first, row(gain_first), row(offset_first), row(merge_gain), row(merge_offset),
         scale_second, row(gain_second), row(offset_second),
-        *[jnp.asarray(t) for t in tables()],
+        cut, keep, valid, heads,
     )
+    return jnp.transpose(out.reshape(2, 12, 1, 12, 1024), (1, 2, 0, 3, 4))
 
 
 def solution(mesh):

time: 56.7 us -> 62.5 us (1.10)
  local copies, waits for them, and re-layouts: 5.66 us -> 13.6 us
  Pallas kernels: 50.7 us -> 48.5 us
    unnamed x35 -> x28, local copies, waits for them, and re-layouts: 3.11 us -> 11.1 us
    pallas_call x1, Pallas kernels: 50.7 us -> 48.5 us  [body(): pl.pallas_call(functools.partial(kernel, nlat, nlon), out_shape=jax.Shape...]
where the time goes in v2:
time: 62.5 us; the launch traced here: 62 us
  Pallas kernels  48.5 us (78%)
  local copies, waits for them, and re-layouts  13.6 us (22%)
    pallas_call x1, Pallas kernels, body(): pl.pallas_call(functools.partial(kernel, nlat, nlon), out_shape=jax.Shape...  48.5 us
    unnamed x28, local copies, waits for them, and re-layouts  11.1 us
    pallas_call x1, local copies, waits for them, and re-layouts, body(): pl.pallas_call(functools.partial(kernel, nlat, nlon), out_shape=jax.Shape...  2.49 us

profile of v2, /device:TPU:1, one launch (start us, length us, event | category | flops | bytes accessed | tf_op | source)
XLA Modules:
  0.0 62.0 jit_solution(5580628992669165094)
XLA Ops:
  0.0 0.0 copy-start
  0.0 1.0 %copy-done = bf16[512,512]{1,0:T(8,128)(2,1)S(1)} copy-done((bf16[512,512]{1,0:T(8,128)(2,1)S(1)}, bf16[512,512]{1,0:T(8,128)(2,1)}, u32[]{:S(2)}) %copy-start) | copy-done | bytes 524312
  1.0 0.0 copy-start.1
  1.0 0.7 %copy-done.1 = f32[1024]{0:T(1024)S(1)} copy-done((f32[1024]{0:T(1024)S(1)}, f32[1024]{0:T(1024)}, u32[]{:S(2)}) %copy-start.1) | copy-done | bytes 4120
  1.7 0.0 copy-start.2
  1.7 0.7 %copy-done.2 = f32[1024]{0:T(1024)S(1)} copy-done((f32[1024]{0:T(1024)S(1)}, f32[1024]{0:T(1024)}, u32[]{:S(2)}) %copy-start.2) | copy-done | bytes 4120
  2.4 0.0 copy-start.3
  2.4 0.7 %copy-done.3 = f32[1024]{0:T(1024)S(1)} copy-done((f32[1024]{0:T(1024)S(1)}, f32[1024]{0:T(1024)}, u32[]{:S(2)}) %copy-start.3) | copy-done | bytes 4120
  3.1 0.0 copy-start.4
  3.1 0.7 %copy-done.4 = f32[1024]{0:T(1024)S(1)} copy-done((f32[1024]{0:T(1024)S(1)}, f32[1024]{0:T(1024)}, u32[]{:S(2)}) %copy-start.4) | copy-done | bytes 4120
  3.8 0.0 copy-start.5
  3.8 0.7 %copy-done.5 = f32[512]{0:T(512)S(1)} copy-done((f32[512]{0:T(512)S(1)}, f32[512]{0:T(512)}, u32[]{:S(2)}) %copy-start.5) | copy-done | bytes 2072
  4.5 0.0 copy-start.6
  4.5 0.7 %copy-done.6 = f32[512]{0:T(512)S(1)} copy-done((f32[512]{0:T(512)S(1)}, f32[512]{0:T(512)}, u32[]{:S(2)}) %copy-start.6) | copy-done | bytes 2072
  5.2 0.0 copy-start.7
  5.2 0.7 %copy-done.7 = f32[8]{0:T(128)S(1)} copy-done((f32[8]{0:T(128)S(1)}, f32[8]{0:T(128)}, u32[]{:S(2)}) %copy-start.7) | copy-done | bytes 56
  5.8 0.0 copy-start.8
  5.8 0.7 %copy-done.8 = f32[8]{0:T(128)S(1)} copy-done((f32[8]{0:T(128)S(1)}, f32[8]{0:T(128)}, u32[]{:S(2)}) %copy-start.8) | copy-done | bytes 56
  6.5 0.0 copy-start.9
  6.5 1.0 %copy-done.9 = bf16[4,160,160]{2,1,0:T(8,128)(2,1)S(1)} copy-done((bf16[4,160,160]{2,1,0:T(8,128)(2,1)S(1)}, bf16[4,160,160]{2,1,0:T(8,128)(2,1)}, u32[]{:S(2)}) %copy-start.9) | copy-done | bytes 204824
  7.4 0.0 copy-start.10
  7.4 0.9 %copy-done.10 = bf16[320,320]{1,0:T(8,128)(2,1)S(1)} copy-done((bf16[320,320]{1,0:T(8,128)(2,1)S(1)}, bf16[320,320]{1,0:T(8,128)(2,1)}, u32[]{:S(2)}) %copy-start.10) | copy-done | bytes 204824
  8.4 0.0 copy-start.11
  8.4 0.9 %copy-done.11 = bf16[2,160,192]{2,1,0:T(8,128)(2,1)S(1)} copy-done((bf16[2,160,192]{2,1,0:T(8,128)(2,1)S(1)}, bf16[2,160,192]{2,1,0:T(8,128)(2,1)}, u32[]{:S(2)}) %copy-start.11) | copy-done | bytes 122904
  9.3 0.0 copy-start.12
  9.3 0.9 %copy-done.12 = bf16[256,256]{1,0:T(8,128)(2,1)S(1)} copy-done((bf16[256,256]{1,0:T(8,128)(2,1)S(1)}, bf16[256,256]{1,0:T(8,128)(2,1)}, u32[]{:S(2)}) %copy-start.12) | copy-done | bytes 131096
  10.2 0.0 copy-start.13
  10.2 0.9 %copy-done.13 = f32[160,128]{1,0:T(8,128)S(1)} copy-done((f32[160,128]{1,0:T(8,128)S(1)}, f32[160,128]{1,0:T(8,128)}, u32[]{:S(2)}) %copy-start.13) | copy-done | bytes 81944
  11.1 48.5 %shard_map.208 = bf16[2,144,1024]{2,1,0:T(8,128)(2,1)} custom-call(bf16[4,12,24,512]{3,2,1,0:T(8,128)(2,1)} %bitcast.18, bf16[512,1536]{1,0:T(8,128)(2,1)} %packed1_hbm.1, bf16[512,512]{1,0:T(8,128)(2,1)S(1)} %copy-done, bf16[2048,1024]{1,0:T(8,128)(2,1)} %merge_hbm.1, bf16[1024,1536]{1,0:T(8,128)(2,1)} %packed2_hbm.1, bf16[512,1024]{1,0:T(8,128)(2,1)} %out2_hbm.1, ...), custom_call_target="tpu_custom_call" | custom-call | flops 6000000000 | bytes 14000000 | tf_op jit(solution)/shard_map/pallas_call | solution.py:364
  59.6 2.5 %copy.24 = bf16[2,144,1024]{2,0,1:T(2,128)(2,1)} copy(bf16[2,144,1024]{2,1,0:T(8,128)(2,1)} %shard_map.208) | data formatting | bytes 1179648 | tf_op jit(solution)/shard_map/pallas_call | solution.py:364
Async XLA Ops:
  0.0 1.0 %copy-start = (bf16[512,512]{1,0:T(8,128)(2,1)S(1)}, bf16[512,512]{1,0:T(8,128)(2,1)}, u32[]{:S(2)}) copy-start(bf16[512,512]{1,0:T(8,128)(2,1)} %out1_hbm.1) | copy-start | bytes 1572868
  1.0 0.7 %copy-start.1 = (f32[1024]{0:T(1024)S(1)}, f32[1024]{0:T(1024)}, u32[]{:S(2)}) copy-start(f32[1024]{0:T(1024)} %param.29) | copy-start | bytes 12292
  1.7 0.7 %copy-start.2 = (f32[1024]{0:T(1024)S(1)}, f32[1024]{0:T(1024)}, u32[]{:S(2)}) copy-start(f32[1024]{0:T(1024)} %param.30) | copy-start | bytes 12292
  2.4 0.7 %copy-start.3 = (f32[1024]{0:T(1024)S(1)}, f32[1024]{0:T(1024)}, u32[]{:S(2)}) copy-start(f32[1024]{0:T(1024)} %param.34) | copy-start | bytes 12292
  3.1 0.7 %copy-start.4 = (f32[1024]{0:T(1024)S(1)}, f32[1024]{0:T(1024)}, u32[]{:S(2)}) copy-start(f32[1024]{0:T(1024)} %param.35) | copy-start | bytes 12292
  3.8 0.7 %copy-start.5 = (f32[512]{0:T(512)S(1)}, f32[512]{0:T(512)}, u32[]{:S(2)}) copy-start(f32[512]{0:T(512)} %param.26) | copy-start | bytes 6148
  4.5 0.7 %copy-start.6 = (f32[512]{0:T(512)S(1)}, f32[512]{0:T(512)}, u32[]{:S(2)}) copy-start(f32[512]{0:T(512)} %param.27) | copy-start | bytes 6148
  5.2 0.7 %copy-start.7 = (f32[8]{0:T(128)S(1)}, f32[8]{0:T(128)}, u32[]{:S(2)}) copy-start(f32[8]{0:T(128)} %scale1.1) | copy-start | bytes 100
  5.8 0.7 %copy-start.8 = (f32[8]{0:T(128)S(1)}, f32[8]{0:T(128)}, u32[]{:S(2)}) copy-start(f32[8]{0:T(128)} %scale2.1) | copy-start | bytes 100
  6.5 1.0 %copy-start.9 = (bf16[4,160,160]{2,1,0:T(8,128)(2,1)S(1)}, bf16[4,160,160]{2,1,0:T(8,128)(2,1)}, u32[]{:S(2)}) copy-start(bf16[4,160,160]{2,1,0:T(8,128)(2,1)} %constant.21.clone.keep) | copy-start | bytes 614404
  7.4 0.9 %copy-start.10 = (bf16[320,320]{1,0:T(8,128)(2,1)S(1)}, bf16[320,320]{1,0:T(8,128)(2,1)}, u32[]{:S(2)}) copy-start(bf16[320,320]{1,0:T(8,128)(2,1)} %constant.17.clone.pick_hbm) | copy-start | bytes 614404
  8.4 0.9 %copy-start.11 = (bf16[2,160,192]{2,1,0:T(8,128)(2,1)S(1)}, bf16[2,160,192]{2,1,0:T(8,128)(2,1)}, u32[]{:S(2)}) copy-start(bf16[2,160,192]{2,1,0:T(8,128)(2,1)} %constant.16.clone.cut) | copy-start | bytes 368644
  9.3 0.9 %copy-start.12 = (bf16[256,256]{1,0:T(8,128)(2,1)S(1)}, bf16[256,256]{1,0:T(8,128)(2,1)}, u32[]{:S(2)}) copy-start(bf16[256,256]{1,0:T(8,128)(2,1)} %constant.23.clone.heads) | copy-start | bytes 393220
  10.2 0.9 %copy-start.13 = (f32[160,128]{1,0:T(8,128)S(1)}, f32[160,128]{1,0:T(8,128)}, u32[]{:S(2)}) copy-start(f32[160,128]{1,0:T(8,128)} %constant.22.clone.valid) | copy-start | bytes 245764

commit v3 on v2

--- a/solution.py
+++ b/solution.py
@@ -130,10 +130,11 @@
     nlat, nlon,
     feat_hbm, packed1_hbm, out1_hbm, merge_hbm, packed2_hbm, out2_hbm,
     pick_hbm, late_hbm, early_hbm, place_hbm,
-    scale1, gain1, offset1, gainm, offsetm, scale2, gain2, offset2,
-    cut, keep, valid, heads,
+    scale1_hbm, gain1_hbm, offset1_hbm, gainm_hbm, offsetm_hbm, scale2_hbm, gain2_hbm, offset2_hbm,
+    cut_hbm, keep_hbm, valid_hbm, heads_hbm,
     out,
     feat, packed1, wout1, wmerge, packed2, wout2, pick, late, early, place,
+    scale1, gain1, offset1, gainm, offsetm, scale2, gain2, offset2, cut, keep, valid, heads,
     send0, sendr, x, yn, ctx, first, picked, mb, quarter, t0, t1, t2, r0, r1, r2,
     load_sem, s1, v1, s2, v2, s3, v3, s4, v4,
 ):
@@ -150,16 +151,28 @@
             device_id=where, device_id_type=MESH,
         )
 
-    loads = [
-        pltpu.make_async_copy(a, b, load_sem.at[n])
-        for n, (a, b) in enumerate(
-            [(feat_hbm, feat), (packed1_hbm, packed1), (out1_hbm, wout1),
-             (merge_hbm, wmerge), (packed2_hbm, packed2), (out2_hbm, wout2),
-             (pick_hbm, pick), (late_hbm, late), (early_hbm, early), (place_hbm, place)]
-        )
-    ]
-    for load in loads:
-        load.start()
+    def load(*pairs):
+        copies = [pltpu.make_async_copy(a, b, load_sem.at[order.pop()]) for a, b in pairs]
+        for copy in copies:
+            copy.start()
+
+        def wait():
+            for copy in copies:
+                copy.wait()
+
+        return wait
+
+    order = list(range(22))
+    cut_loaded = load((feat_hbm, feat), (cut_hbm, cut))
+    first_loaded = load(
+        (packed1_hbm, packed1), (heads_hbm, heads), (keep_hbm, keep), (valid_hbm, valid), (scale1_hbm, scale1),
+        (out1_hbm, wout1), (gain1_hbm, gain1), (offset1_hbm, offset1),
+    )
+    merge_loaded = load((pick_hbm, pick), (merge_hbm, wmerge), (gainm_hbm, gainm), (offsetm_hbm, offsetm))
+    second_loaded = load(
+        (packed2_hbm, packed2), (out2_hbm, wout2), (scale2_hbm, scale2), (gain2_hbm, gain2), (offset2_hbm, offset2),
+        (late_hbm, late), (early_hbm, early), (place_hbm, place),
+    )
 
     barrier = pltpu.get_barrier_semaphore()
     for dlat, dlon in [
@@ -168,7 +181,7 @@
     ]:
         pl.semaphore_signal(barrier, inc=1, device_id=peer(dlat, dlon), device_id_type=MESH)
 
-    loads[0].wait()
+    cut_loaded()
     pl.semaphore_wait(barrier, jnp.where(even, 11, 9))
 
     feature_copies = [
@@ -203,8 +216,7 @@
             else:
                 x[0, pl.ds(3, 4)] = atoms
 
-    loads[1].wait()
-    loads[2].wait()
+    first_loaded()
     edge = send(first.at[:, pl.ds(0, 1)], first.at[:, pl.ds(8, 1)], s2, v2, peer(-1, 0))
     last_lat = lat == nlat - 1
 
@@ -247,8 +259,7 @@
         send(mb.at[1, 0], quarter.at[2], s3.at[1], v3.at[2], peer(0, -1)),
     ]
     edge.wait_recv()
-    loads[6].wait()
-    loads[3].wait()
+    merge_loaded()
     for half in range(2):
         for cb in range(2):
             fine = first[half, pl.ds(4 * cb + 1, 4)].reshape(320, 512)
@@ -278,13 +289,10 @@
             if half == 1:
                 even_copies[2].wait_recv()
 
-    loads[4].wait()
-    loads[5].wait()
+    second_loaded()
     project(quarter[pl.ds(0, 3)].reshape(240, 1024), packed2, heads, yn, 0, 3)
     even_copies[0].wait_recv()
     project(quarter[3], packed2, heads, yn, 3, 1)
-    for load in loads[7:]:
-        load.wait()
     upper = odd.astype(F32)
     levels = keep[2].astype(F32) * upper + (1.0 - upper)
     final_copies = []
@@ -356,7 +364,6 @@
          packed_second, scale_second, output_second, gain_second, offset_second):
     any_spec = pl.BlockSpec(memory_space=pl.ANY)
     vmem = pl.BlockSpec(memory_space=pltpu.VMEM)
-    smem = pl.BlockSpec(memory_space=pltpu.SMEM)
     dma = pltpu.SemaphoreType.DMA
     row = lambda v: v.reshape(1, -1)
     *small, keep, valid, heads = [jnp.asarray(t) for t in tables()]
@@ -364,7 +371,7 @@
     out = pl.pallas_call(
         functools.partial(kernel, nlat, nlon),
         out_shape=jax.ShapeDtypeStruct((2, 144, 1024), BF16),
-        in_specs=[any_spec] * 10 + [smem] + [vmem] * 4 + [smem] + [vmem] * 2 + [vmem] * 4,
+        in_specs=[any_spec] * 22,
         out_specs=vmem,
         scratch_shapes=[
             pltpu.VMEM((4, 12, 24, 512), BF16),
@@ -377,6 +384,15 @@
             pltpu.VMEM((640, 640), BF16),
             pltpu.VMEM((576, 640), BF16),
             pltpu.VMEM((4, 144, 608), BF16),
+            pltpu.SMEM((8,), F32),
+            *[pltpu.VMEM((1, 512), F32)] * 2,
+            *[pltpu.VMEM((1, 1024), F32)] * 2,
+            pltpu.SMEM((8,), F32),
+            *[pltpu.VMEM((1, 1024), F32)] * 2,
+            pltpu.VMEM((2, 160, 192), BF16),
+            pltpu.VMEM((4, WIN, WIN), BF16),
+            pltpu.VMEM((WIN, 128), F32),
+            pltpu.VMEM((256, 256), BF16),
             pltpu.VMEM((8, 80, 512), BF16),
             pltpu.VMEM((1, 80, 512), BF16),
             pltpu.VMEM((2, 8, 80, 512), BF16),
@@ -392,14 +408,14 @@
             pltpu.VMEM((2, 2, 144, 256), BF16),
             pltpu.VMEM((2, 2, 80, 256), BF16),
             pltpu.VMEM((2, 2, 80, 256), BF16),
-            dma((10,)),
+            dma((22,)),
             dma((6,)), dma((6,)),
             dma, dma,
             dma((3,)), dma((4,)),
             dma((10,)), dma((10,)),
         ],
         compiler_params=pltpu.CompilerParams(
-            collective_id=0, has_side_effects=True, vmem_limit_bytes=52 * 2**20
+            collective_id=0, has_side_effects=True, vmem_limit_bytes=62 * 2**20
         ),
         cost_estimate=pl.CostEstimate(flops=6_000_000_000, bytes_accessed=14_000_000, transcendentals=2_000_000),
     )(

time: 62.5 us -> 50.1 us (0.80)
  local copies, waits for them, and re-layouts: 13.6 us -> 2.49 us
  Pallas kernels: 48.5 us -> 47.5 us
    unnamed x28 -> x0, local copies, waits for them, and re-layouts: 11.1 us -> none
    pallas_call x1, Pallas kernels: 48.5 us -> 47.5 us  [body(): pl.pallas_call(functools.partial(kernel, nlat, nlon), out_shape=jax.Shape...]
where the time goes in v3:
time: 50.1 us; the launch traced here: 50 us
  Pallas kernels  47.5 us (95%)
  local copies, waits for them, and re-layouts  2.49 us (5%)
    pallas_call x1, Pallas kernels, body(): pl.pallas_call(functools.partial(kernel, nlat, nlon), out_shape=jax.Shape...  47.5 us
    pallas_call x1, local copies, waits for them, and re-layouts, body(): pl.pallas_call(functools.partial(kernel, nlat, nlon), out_shape=jax.Shape...  2.49 us

profile of v3, /device:TPU:1, one launch (start us, length us, event | category | flops | bytes accessed | tf_op | source)
XLA Modules:
  0.0 50.0 jit_solution(15535930720161978555)
XLA Ops:
  0.0 47.5 %shard_map.208 = bf16[2,144,1024]{2,1,0:T(8,128)(2,1)} custom-call(bf16[4,12,24,512]{3,2,1,0:T(8,128)(2,1)} %bitcast.12, bf16[512,1536]{1,0:T(8,128)(2,1)} %packed1_hbm.1, bf16[512,512]{1,0:T(8,128)(2,1)} %out1_hbm.1, bf16[2048,1024]{1,0:T(8,128)(2,1)} %merge_hbm.1, bf16[1024,1536]{1,0:T(8,128)(2,1)} %packed2_hbm.1, bf16[512,1024]{1,0:T(8,128)(2,1)} %out2_hbm.1, ...), custom_call_target="tpu_custom_call" | custom-call | flops 6000000000 | bytes 14000000 | tf_op jit(solution)/shard_map/pallas_call | solution.py:371
  47.5 2.5 %copy.24 = bf16[2,144,1024]{2,0,1:T(2,128)(2,1)} copy(bf16[2,144,1024]{2,1,0:T(8,128)(2,1)} %shard_map.208) | data formatting | bytes 1179648 | tf_op jit(solution)/shard_map/pallas_call | solution.py:371

commit v4 on v3

v4 whole, which is shorter than its diff:
```python
import functools

import jax
import jax.numpy as jnp
import numpy as np
from jax import lax
from jax.experimental import pallas as pl
from jax.experimental.pallas import tpu as pltpu
from jax.sharding import PartitionSpec as P

ATOM = 40
CELLS = 36
WIN = 4 * ATOM
MESH = pl.DeviceIdType.MESH
BF16 = jnp.bfloat16
F32 = jnp.float32
LOG2E = 1.4426950408889634
NORM_EPS = 1e-05
UNIT_EPS = 1e-06


def level_of(p, j):
    return (2 * p + j + 1) % 4


@functools.lru_cache(None)
def tables():
    cut = np.zeros((2, 160, 192), np.float32)
    for part in range(2):
        for hb in range(4):
            for i in range(3):
                for j in range(2):
                    for c in range(6):
                        row = hb * 40 + (i * 2 + j) * 6 + c
                        cut[part, row, (j * 6 + c) * 16 + 3 * hb + i + 4 * part] = 1
    pick = np.zeros((3, 160, 240), np.float32)
    for cp in range(2):
        for rp in range(2):
            for u in range(2):
                for i in range(3):
                    for j in range(2):
                        for c in range(3):
                            row = (cp * 2 + rp) * 40 + u * 18 + (i * 2 + j) * 3 + c
                            fine = 6 * u + 2 * i + rp
                            hb, at = 1 + fine // 3, (fine % 3 * 2 + j) * 6 + 2 * c + cp
                            pick[0, row, hb * 40 + at] = 1
                            for p in range(2):
                                pick[1 + p, row, (hb * 40 if hb < 4 else 160 + p * 40) + at] = 1
    late = np.zeros((320, 320), np.float32)
    early = np.zeros((288, 320), np.float32)
    for lane in range(4):
        for u in range(2):
            for j in range(2):
                for i in range(3):
                    for c in range(6):
                        src = lane * 80 + c // 3 * 40 + u * 18 + (i * 2 + j) * 3 + c % 3
                        late[(u * 2 + j) * 80 + lane * 18 + i * 6 + c, src] = 1
                        early[j * 144 + lane * 36 + u * 18 + i * 6 + c, src] = 1
    place = np.zeros((4, 144, 608), np.float32)
    for lane in range(4):
        for row in range(12):
            for col in range(12):
                half, c = (1, col) if col < 6 else (0, col - 6)
                if row < 3:
                    src = 448 + 80 * half + lane * 18 + row * 6 + c
                elif row < 9:
                    src = 144 * half + lane * 36 + (row - 3) * 6 + c
                else:
                    src = 288 + 80 * half + lane * 18 + (row - 9) * 6 + c
                place[lane, row * 12 + col, src] = 1
    t = np.arange(WIN) % ATOM
    atom = np.arange(WIN) // ATOM
    keep = np.stack(
        [
            (t // 6 % 2)[:, None] == (t // 6 % 2)[None],
            (atom % 2)[:, None] == (atom % 2)[None],
            (t % 18 // 3 % 2)[:, None] == (t % 18 // 3 % 2)[None],
            (t < 18)[:, None] == (t < 18)[None],
        ]
    ).astype(np.float32)
    valid = np.broadcast_to((t < CELLS)[:, None], (WIN, 128)).astype(np.float32)
    low = (np.arange(128) < 64)[None].astype(np.float32)
    sides = np.stack([valid * low, valid * (1 - low)])
    group = np.arange(256) // 64
    heads = (group[:, None] == group[None]).astype(np.float32)
    b = lambda x: x.astype(jnp.bfloat16)
    return b(cut), b(pick), b(late), b(early), b(place), b(keep), b(sides), b(heads)


def layer_norm(values, gain, offset):
    average = jnp.mean(values, axis=-1, keepdims=True)
    centred = values - average
    spread = jnp.mean(centred * centred, axis=-1, keepdims=True)
    return centred * lax.rsqrt(spread + NORM_EPS) * gain + offset


def dot(a, b):
    return jnp.dot(a, b, preferred_element_type=F32)


def project(x, weight_ref, heads_ref, store):
    for at in range(3):
        y = dot(x, weight_ref[:, pl.ds(512 * at, 512)]).astype(BF16)
        if at < 2:
            squares = y * y
            total = jnp.concatenate(
                [dot(squares[:, :256], heads_ref[...]), dot(squares[:, 256:], heads_ref[...])], axis=1
            )
            y = (y.astype(F32) * lax.rsqrt(total + UNIT_EPS)).astype(BF16)
        store(512 * at, y)


def attend(fetch, store, mask, sides_ref, scale_ref):
    low = lax.broadcasted_iota(jnp.int32, (WIN, 128), 1) < 64
    for g in range(4):
        q, k, v = fetch(128 * g), fetch(512 + 128 * g), fetch(1024 + 128 * g)
        parts = []
        for side in range(2):
            key = k * sides_ref[side]
            value = v * sides_ref[side] + sides_ref[1 - side]
            score = lax.dot_general(q, key, (((1,), (1,)), ((), ())), preferred_element_type=F32)
            weight = jnp.exp2(score * (scale_ref[2 * g + side] * LOG2E)).astype(BF16)
            parts.append(dot(weight if mask is None else weight * mask, value))
        top = jnp.where(low, parts[0], parts[1])
        total = pltpu.roll(jnp.where(low, parts[1], parts[0]), 64, 1)
        store(128 * g, (top / total).astype(BF16))


def kernel(
    nlat, nlon,
    feat_hbm, packed1_hbm, out1_hbm, merge_hbm, packed2_hbm, out2_hbm,
    pick_hbm, late_hbm, early_hbm, place_hbm,
    scale1_hbm, gain1_hbm, offset1_hbm, gainm_hbm, offsetm_hbm, scale2_hbm, gain2_hbm, offset2_hbm,
    cut_hbm, keep_hbm, sides_hbm, heads_hbm,
    out,
    feat, packed1, wout1, wmerge, packed2, wout2, pick, late, early, place,
    scale1, gain1, offset1, gainm, offsetm, scale2, gain2, offset2, cut, keep, sides, heads,
    send0, send7, send_row, send_corner, x, rim, yn, ctx, first, edge_out, edge_in, picked, mb, quarter, t0, t1, t2, r0, r1, r2,
    load_sem, s1, v1, s2, v2, s3, v3, s4, v4,
):
    lat, lon = lax.axis_index("lat"), lax.axis_index("lon")
    odd = lax.rem(lon, 2)
    even = odd == 0

    def peer(dlat, dlon):
        return (lax.rem(lat + dlat + nlat, nlat), lax.rem(lon + dlon + nlon, nlon))

    def send(src, dst, send_sem, recv_sem, where):
        return pltpu.make_async_remote_copy(
            src_ref=src, dst_ref=dst, send_sem=send_sem, recv_sem=recv_sem,
            device_id=where, device_id_type=MESH,
        )

    def load(*pairs):
        copies = [pltpu.make_async_copy(a, b, load_sem.at[order.pop()]) for a, b in pairs]
        for copy in copies:
            copy.start()

        def wait():
            for copy in copies:
                copy.wait()

        return wait

    order = list(range(22))
    cut_loaded = load((feat_hbm, feat), (cut_hbm, cut))
    barrier = pltpu.get_barrier_semaphore()
    for dlat, dlon in [
        (0, 1), (0, -1), (0, -2), (1, 0), (1, 1), (-1, 0), (-1, -1), (-1, -2),
        (0, jnp.where(even, 2, -3)), (-1, jnp.where(even, 1, -3)),
    ]:
        pl.semaphore_signal(barrier, inc=1, device_id=peer(dlat, dlon), device_id_type=MESH)

    first_loaded = load(
        (packed1_hbm, packed1), (heads_hbm, heads), (keep_hbm, keep), (sides_hbm, sides), (scale1_hbm, scale1),
        (out1_hbm, wout1), (gain1_hbm, gain1), (offset1_hbm, offset1),
    )
    merge_loaded = load((pick_hbm, pick), (merge_hbm, wmerge), (gainm_hbm, gainm), (offsetm_hbm, offsetm))
    second_loaded = load(
        (packed2_hbm, packed2), (out2_hbm, wout2), (scale2_hbm, scale2), (gain2_hbm, gain2), (offset2_hbm, offset2),
        (late_hbm, late), (early_hbm, early), (place_hbm, place),
    )

    cut_loaded()

    feature_copies = [
        send(send0.at[n], x.at[n, 1], s1.at[n], v1.at[n], peer(0, -1)) for n in range(3)
    ] + [
        send(send7, rim.at[1, 0], s1.at[3], v1.at[3], peer(0, -1)),
        send(send_corner, rim.at[1, 1], s1.at[4], v1.at[4], peer(-1, -1)),
        send(send_row, rim.at[0, 1], s1.at[5], v1.at[5], peer(-1, 0)),
    ]

    def atoms_of(half, p, part):
        tokens = jnp.stack([
            feat[level_of(p, j), 6 * half : 6 * half + 6].astype(F32)[:, 8 * part : 8 * part + 16]
            for j in range(2)
        ]).astype(BF16).reshape(192, 512)
        return dot(cut[part], tokens).reshape(4, ATOM, 512)

    for half in range(2):
        upper = [atoms_of(half, p, 0) for p in range(2)]
        if half == 0:
            for p in range(2):
                send0[0, p] = upper[p][1:3].reshape(80, 512).astype(BF16)
            pl.semaphore_wait(barrier, jnp.where(even, 11, 9))
            feature_copies[0].start()
        lower = [atoms_of(half, p, 1) for p in range(2)]
        ends = [jnp.concatenate([a[n] for a in side], axis=0).astype(BF16) for side, n in ((upper, 0), (lower, 3))]
        for p in range(2):
            second = jnp.concatenate([upper[p][3], lower[p][0]], axis=0).astype(BF16)
            third = lower[p][1:3].reshape(80, 512).astype(BF16)
            if half == 0:
                send0[1, p] = second
                send0[2, p] = third
            else:
                x[0, 0, p] = upper[p][1:3].reshape(80, 512).astype(BF16)
                x[1, 0, p] = second
                x[2, 0, p] = third
        if half == 0:
            send7[...] = ends[1]
            send_corner[...] = ends[0]
            for copy in feature_copies[1:5]:
                copy.start()
        else:
            send_row[...] = ends[0]
            feature_copies[5].start()
            rim[0, 0] = ends[1]

    first_loaded()
    edge = send(edge_out, edge_in, s2, v2, peer(-1, 0))
    last_lat = lat == nlat - 1

    even_copies = [
        [
            send(mb.at[cb, 0, 0], quarter.at[cb, 3], s3.at[cb, 0], v3.at[cb, 3], peer(0, -2)),
            send(mb.at[cb, 0, 1], quarter.at[cb, 3], s3.at[cb, 1], v3.at[cb, 3], peer(0, -1)),
            send(mb.at[cb, 1, 1], quarter.at[cb, 0], s3.at[cb, 2], v3.at[cb, 0], peer(0, 1)),
        ]
        for cb in range(2)
    ]
    odd_copies = [
        [
            send(mb.at[cb, 0, 0], quarter.at[cb, 1], s3.at[cb, 0], v3.at[cb, 1], peer(0, -1)),
            send(mb.at[cb, 1, 0], quarter.at[cb, 2], s3.at[cb, 1], v3.at[cb, 2], peer(0, -1)),
        ]
        for cb in range(2)
    ]

    def merge(cb):
        for half in range(2):
            parts = []
            for p in range(2):
                if cb == 0:
                    moved = dot(pick[0], first[0:3, half, p].reshape(240, 512))
                else:
                    fine = jnp.concatenate([first[2:4, half, p].reshape(160, 512), edge_in[half]], axis=0)
                    moved = dot(pick[1 + p], fine)
                parts.append(moved.reshape(4, ATOM, 512))
            parts = jnp.concatenate(parts, axis=1).astype(BF16)
            for at in range(4):
                picked[cb, pl.ds(80 * half, 80), pl.ds(512 * at, 512)] = parts[at]
        normed = layer_norm(dot(picked[cb], wmerge[...]), gainm[...], offsetm[...])
        for half in range(2):
            for p in range(2):
                rows = normed[(half * 2 + p) * ATOM : (half * 2 + p + 1) * ATOM]
                mb[cb, half, p] = jnp.concatenate([rows[:, :512], rows[:, 512:]], axis=0).astype(BF16)

        @pl.when(even)
        def _():
            for copy in even_copies[cb]:
                copy.start()
            quarter[cb, 0] = mb[cb, 1, 0]

        @pl.when(jnp.logical_not(even))
        def _():
            for copy in odd_copies[cb]:
                copy.start()
            quarter[cb, 1] = mb[cb, 0, 1]
            quarter[cb, 2] = mb[cb, 1, 1]

    def merged_arrived(cb):
        @pl.when(even)
        def _():
            odd_copies[cb][0].wait_recv()
            odd_copies[cb][1].wait_recv()

        @pl.when(jnp.logical_not(even))
        def _():
            even_copies[cb][2].wait_recv()

        even_copies[cb][0].wait_recv()

    def band(b, carry):
        for n in range(3):
            @pl.when(b == n)
            def _():
                feature_copies[n].wait_recv()

        @pl.when(b == 3)
        def _():
            for n in range(3, 6):
                feature_copies[n].wait_recv()
            for half in range(2):
                near, far = rim[half, 0].astype(F32), rim[half, 1].astype(F32)
                for p in range(2):
                    rows = slice(ATOM * p, ATOM * p + ATOM)
                    x[3, half, p] = jnp.concatenate([near[rows], far[rows]], axis=0).astype(BF16)

        xb = x[b].reshape(320, 512)

        def keep_rows(at, y):
            yn[:, :, :, pl.ds(at, 512)] = y.reshape(2, 2, 80, 512)

        project(xb, packed1, heads, keep_rows)
        wrapped = jnp.where(jnp.logical_and(last_lat, b == 3), 1.0, 0.0).astype(F32)
        rows = keep[1].astype(F32) * wrapped + (1.0 - wrapped)
        for p in range(2):
            def fetch(at):
                return yn[:, p, :, pl.ds(at, 128)].reshape(WIN, 128)

            def keep_context(at, value):
                ctx[:, p, :, pl.ds(at, 128)] = value.reshape(2, 80, 128)

            mask = rows if p == 0 else rows * keep[0].astype(F32)
            attend(fetch, keep_context, mask.astype(BF16), sides, scale1)
        branch = layer_norm(dot(ctx[...].reshape(320, 512), wout1[...]), gain1[...], offset1[...])
        result = (xb.astype(F32) + branch).reshape(2, 2, 80, 512)
        first[b] = result.astype(BF16)

        @pl.when(b == 0)
        def _():
            edge_out[...] = result[:, :, :ATOM].reshape(2, 80, 512).astype(BF16)
            edge.start()

        @pl.when(b == 2)
        def _():
            merge_loaded()
            merge(0)
        return carry

    lax.fori_loop(0, 4, band, 0)

    edge.wait_recv()
    merge(1)

    second_loaded()
    odd_half = odd.astype(F32)
    levels = keep[2].astype(F32) * odd_half + (1.0 - odd_half)

    def keep_rows(at, y):
        yn[0, :, :, pl.ds(at, 512)] = y.reshape(2, 80, 512)

    def fetch(at):
        return yn[0, :, :, pl.ds(at, 128)].reshape(WIN, 128)

    def keep_context(at, value):
        ctx[0, :, :, pl.ds(at, 128)] = value.reshape(2, 80, 128)

    final_copies = []
    for cb in range(2):
        merged_arrived(cb)
        if cb == 1:
            wrapped = jnp.where(last_lat, 1.0, 0.0).astype(F32)
            mask = levels * (keep[3].astype(F32) * wrapped + (1.0 - wrapped))
        else:
            mask = levels
        own = [quarter[cb, n].astype(F32) for n in range(4)]
        own = jnp.concatenate([jnp.concatenate([q[:ATOM], q[ATOM:]], axis=1) for q in own], axis=0)
        project(own.astype(BF16), packed2, heads, keep_rows)
        attend(fetch, keep_context, mask.astype(BF16), sides, scale2)
        for half in (1, 0):
            branch = layer_norm(dot(ctx[0, half], wout2[...]), gain2[...], offset2[...])
            second = (own[80 * half : 80 * half + 80] + branch).astype(BF16)
            stacked = jnp.concatenate([second[:, 256 * n : 256 * n + 256] for n in range(4)], axis=0)
            if cb == 1:
                units = dot(late[...], stacked).astype(BF16).reshape(2, 2, 80, 256)
                if half == 0:
                    r1[0, 0] = units[0, 0]
                t1[half] = units[0]
                t2[half] = units[1]
            else:
                units = dot(early[...], stacked).astype(BF16).reshape(2, 144, 256)
                if half == 0:
                    r0[0, 0] = units[0]
                t0[half] = units
            for j in range(2):
                to = 2 * half + (0 if j == 0 else 1 - 2 * odd)
                n = half * 2 + j
                if cb == 1:
                    final_copies.append(
                        send(t2.at[half, j], r2.at[half, j], s4.at[n], v4.at[n], peer(1, to)))
                    final_copies[-1].start()
                if n > 0:
                    src, dst, base = (t1, r1, 3) if cb == 1 else (t0, r0, 6)
                    final_copies.append(
                        send(src.at[half, j], dst.at[half, j], s4.at[base + n], v4.at[base + n], peer(0, to)))
                    final_copies[-1].start()

    for copy in final_copies:
        copy.wait_recv()
    for level in range(2):
        j = 1 - level
        parts = [r[half, j] for r in (r0, r1, r2) for half in range(2)]
        parts = jnp.concatenate(parts, axis=0)
        for n in range(4):
            out[level, :, pl.ds(256 * n, 256)] = dot(place[n], parts).astype(BF16)

    for copy in feature_copies:
        copy.wait_send()
    edge.wait_send()

    @pl.when(even)
    def _():
        for copy in even_copies[0] + even_copies[1]:
            copy.wait_send()

    @pl.when(jnp.logical_not(even))
    def _():
        for copy in odd_copies[0] + odd_copies[1]:
            copy.wait_send()

    for copy in final_copies:
        copy.wait_send()


def body(nlat, nlon, features, packed_first, scale_first, output_first, gain_first, offset_first,
         merge_weight, merge_gain, merge_offset,
         packed_second, scale_second, output_second, gain_second, offset_second):
    any_spec = pl.BlockSpec(memory_space=pl.ANY)
    vmem = pl.BlockSpec(memory_space=pltpu.VMEM)
    dma = pltpu.SemaphoreType.DMA
    row = lambda v: v.reshape(1, -1)
    *small, keep, sides, heads = [jnp.asarray(t) for t in tables()]
    cut, pick, late, early, place = small
    out = pl.pallas_call(
        functools.partial(kernel, nlat, nlon),
        out_shape=jax.ShapeDtypeStruct((2, 144, 1024), BF16),
        in_specs=[any_spec] * 22,
        out_specs=vmem,
        scratch_shapes=[
            pltpu.VMEM((4, 12, 24, 512), BF16),
            pltpu.VMEM((512, 1536), BF16),
            pltpu.VMEM((512, 512), BF16),
            pltpu.VMEM((2048, 1024), BF16),
            pltpu.VMEM((1024, 1536), BF16),
            pltpu.VMEM((512, 1024), BF16),
            pltpu.VMEM((3, 160, 240), BF16),
            pltpu.VMEM((320, 320), BF16),
            pltpu.VMEM((288, 320), BF16),
            pltpu.VMEM((4, 144, 608), BF16),
            pltpu.SMEM((8,), F32),
            *[pltpu.VMEM((1, 512), F32)] * 2,
            *[pltpu.VMEM((1, 1024), F32)] * 2,
            pltpu.SMEM((8,), F32),
            *[pltpu.VMEM((1, 1024), F32)] * 2,
            pltpu.VMEM((2, 160, 192), BF16),
            pltpu.VMEM((4, WIN, WIN), BF16),
            pltpu.VMEM((2, WIN, 128), BF16),
            pltpu.VMEM((256, 256), BF16),
            pltpu.VMEM((3, 2, 80, 512), BF16),
            pltpu.VMEM((80, 512), BF16),
            pltpu.VMEM((80, 512), BF16),
            pltpu.VMEM((80, 512), BF16),
            pltpu.VMEM((4, 2, 2, 80, 512), BF16),
            pltpu.VMEM((2, 2, 80, 512), BF16),
            pltpu.VMEM((2, 2, 80, 1536), BF16),
            pltpu.VMEM((2, 2, 80, 512), BF16),
            pltpu.VMEM((4, 2, 2, 80, 512), BF16),
            pltpu.VMEM((2, 80, 512), BF16),
            pltpu.VMEM((2, 80, 512), BF16),
            pltpu.VMEM((2, 160, 2048), BF16),
            pltpu.VMEM((2, 2, 2, 80, 512), BF16),
            pltpu.VMEM((2, 4, 80, 512), BF16),
            pltpu.VMEM((2, 2, 144, 256), BF16),
            pltpu.VMEM((2, 2, 80, 256), BF16),
            pltpu.VMEM((2, 2, 80, 256), BF16),
            pltpu.VMEM((2, 2, 144, 256), BF16),
            pltpu.VMEM((2, 2, 80, 256), BF16),
            pltpu.VMEM((2, 2, 80, 256), BF16),
            dma((22,)),
            dma((6,)), dma((6,)),
            dma, dma,
            dma((2, 3)), dma((2, 4)),
            dma((10,)), dma((10,)),
        ],
        compiler_params=pltpu.CompilerParams(
            collective_id=0, has_side_effects=True, vmem_limit_bytes=62 * 2**20
        ),
        cost_estimate=pl.CostEstimate(flops=6_000_000_000, bytes_accessed=14_000_000, transcendentals=2_000_000),
    )(
        jnp.transpose(features, (0, 2, 1, 3)), packed_first, output_first, merge_weight, packed_second, output_second,
        pick, late, early, place,
        scale_first, row(gain_first), row(offset_first), row(merge_gain), row(merge_offset),
        scale_second, row(gain_second), row(offset_second),
        cut, keep, sides, heads,
    )
    return jnp.transpose(out.reshape(2, 12, 1, 12, 1024), (1, 2, 0, 3, 4))


def solution(mesh):
    return jax.shard_map(
        functools.partial(body, mesh.shape["lat"], mesh.shape["lon"]),
        mesh=mesh,
        in_specs=(P(None, "lat", "lon", None),) + (P(),) * 13,
        out_specs=P("lat", "lon", None, None, None),
        check_vma=False,
    )
```

time: 50.1 us -> 46 us (0.918)
  Pallas kernels: 47.5 us -> 43.4 us
    pallas_call x1, Pallas kernels: 47.5 us -> 43.4 us  [body(): pl.pallas_call(functools.partial(kernel, nlat, nlon), out_shape=jax.Shape...]
where the time goes in v4:
time: 46 us; the launch traced here: 45.9 us
  Pallas kernels  43.4 us (94%)
  local copies, waits for them, and re-layouts  2.49 us (5%)
    pallas_call x1, Pallas kernels, body(): pl.pallas_call(functools.partial(kernel, nlat, nlon), out_shape=jax.Shape...  43.4 us
    pallas_call x1, local copies, waits for them, and re-layouts, body(): pl.pallas_call(functools.partial(kernel, nlat, nlon), out_shape=jax.Shape...  2.49 us

profile of v4, /device:TPU:1, one launch (start us, length us, event | category | flops | bytes accessed | tf_op | source)
XLA Modules:
  0.0 45.9 jit_solution(11687381684262487212)
XLA Ops:
  0.0 43.4 %shard_map.208 = bf16[2,144,1024]{2,1,0:T(8,128)(2,1)} custom-call(bf16[4,12,24,512]{3,2,1,0:T(8,128)(2,1)} %bitcast.12, bf16[512,1536]{1,0:T(8,128)(2,1)} %packed1_hbm.1, bf16[512,512]{1,0:T(8,128)(2,1)} %out1_hbm.1, bf16[2048,1024]{1,0:T(8,128)(2,1)} %merge_hbm.1, bf16[1024,1536]{1,0:T(8,128)(2,1)} %packed2_hbm.1, bf16[512,1024]{1,0:T(8,128)(2,1)} %out2_hbm.1, ...), custom_call_target="tpu_custom_call" | custom-call | flops 6000000000 | bytes 14000000 | tf_op jit(solution)/shard_map/pallas_call | solution.py:436
  43.4 2.5 %copy.24 = bf16[2,144,1024]{2,0,1:T(2,128)(2,1)} copy(bf16[2,144,1024]{2,1,0:T(8,128)(2,1)} %shard_map.208) | data formatting | bytes 1179648 | tf_op jit(solution)/shard_map/pallas_call | solution.py:436

commit v5 on v4

--- a/solution.py
+++ b/solution.py
@@ -331,6 +331,9 @@
         @pl.when(b == 0)
         def _():
             edge_out[...] = result[:, :, :ATOM].reshape(2, 80, 512).astype(BF16)
+
+        @pl.when(b == 1)
+        def _():
             edge.start()
 
         @pl.when(b == 2)

time: 46 us -> 45.4 us (0.987)
  Pallas kernels: 43.4 us -> 42.7 us
    pallas_call x1, Pallas kernels: 43.4 us -> 42.7 us  [body(): pl.pallas_call(functools.partial(kernel, nlat, nlon), out_shape=jax.Shape...]
where the time goes in v5:
time: 45.4 us; the launch traced here: 45.2 us
  Pallas kernels  42.7 us (94%)
  local copies, waits for them, and re-layouts  2.49 us (5%)
    pallas_call x1, Pallas kernels, body(): pl.pallas_call(functools.partial(kernel, nlat, nlon), out_shape=jax.Shape...  42.7 us
    pallas_call x1, local copies, waits for them, and re-layouts, body(): pl.pallas_call(functools.partial(kernel, nlat, nlon), out_shape=jax.Shape...  2.49 us

profile of v5, /device:TPU:1, one launch (start us, length us, event | category | flops | bytes accessed | tf_op | source)
XLA Modules:
  0.0 45.2 jit_solution(9965032851620393825)
XLA Ops:
  0.0 42.7 %shard_map.208 = bf16[2,144,1024]{2,1,0:T(8,128)(2,1)} custom-call(bf16[4,12,24,512]{3,2,1,0:T(8,128)(2,1)} %bitcast.12, bf16[512,1536]{1,0:T(8,128)(2,1)} %packed1_hbm.1, bf16[512,512]{1,0:T(8,128)(2,1)} %out1_hbm.1, bf16[2048,1024]{1,0:T(8,128)(2,1)} %merge_hbm.1, bf16[1024,1536]{1,0:T(8,128)(2,1)} %packed2_hbm.1, bf16[512,1024]{1,0:T(8,128)(2,1)} %out2_hbm.1, ...), custom_call_target="tpu_custom_call" | custom-call | flops 6000000000 | bytes 14000000 | tf_op jit(solution)/shard_map/pallas_call | solution.py:439
  42.8 2.5 %copy.24 = bf16[2,144,1024]{2,0,1:T(2,128)(2,1)} copy(bf16[2,144,1024]{2,1,0:T(8,128)(2,1)} %shard_map.208) | data formatting | bytes 1179648 | tf_op jit(solution)/shard_map/pallas_call | solution.py:439

commit v6 on v5

--- a/solution.py
+++ b/solution.py
@@ -98,7 +98,15 @@
     return jnp.dot(a, b, preferred_element_type=F32)
 
 
-def project(x, weight_ref, heads_ref, store):
+def head_scales(scale_ref):
+    head = lax.broadcasted_iota(jnp.int32, (1, 512), 1) // 64
+    factors = jnp.zeros((1, 512), F32)
+    for h in range(8):
+        factors = jnp.where(head == h, scale_ref[h] * LOG2E, factors)
+    return factors
+
+
+def project(x, weight_ref, heads_ref, factors, store):
     for at in range(3):
         y = dot(x, weight_ref[:, pl.ds(512 * at, 512)]).astype(BF16)
         if at < 2:
@@ -106,11 +114,12 @@
             total = jnp.concatenate(
                 [dot(squares[:, :256], heads_ref[...]), dot(squares[:, 256:], heads_ref[...])], axis=1
             )
-            y = (y.astype(F32) * lax.rsqrt(total + UNIT_EPS)).astype(BF16)
+            inverse = lax.rsqrt(total + UNIT_EPS)
+            y = (y.astype(F32) * (inverse * factors if at == 0 else inverse)).astype(BF16)
         store(512 * at, y)
 
 
-def attend(fetch, store, mask, sides_ref, scale_ref):
+def attend(fetch, store, mask, sides_ref):
     low = lax.broadcasted_iota(jnp.int32, (WIN, 128), 1) < 64
     for g in range(4):
         q, k, v = fetch(128 * g), fetch(512 + 128 * g), fetch(1024 + 128 * g)
@@ -119,7 +128,7 @@
             key = k * sides_ref[side]
             value = v * sides_ref[side] + sides_ref[1 - side]
             score = lax.dot_general(q, key, (((1,), (1,)), ((), ())), preferred_element_type=F32)
-            weight = jnp.exp2(score * (scale_ref[2 * g + side] * LOG2E)).astype(BF16)
+            weight = jnp.exp2(score).astype(BF16)
             parts.append(dot(weight if mask is None else weight * mask, value))
         top = jnp.where(low, parts[0], parts[1])
         total = pltpu.roll(jnp.where(low, parts[1], parts[0]), 64, 1)
@@ -228,6 +237,7 @@
             rim[0, 0] = ends[1]
 
     first_loaded()
+    factors1 = head_scales(scale1)
     edge = send(edge_out, edge_in, s2, v2, peer(-1, 0))
     last_lat = lat == nlat - 1
 
@@ -312,7 +322,7 @@
         def keep_rows(at, y):
             yn[:, :, :, pl.ds(at, 512)] = y.reshape(2, 2, 80, 512)
 
-        project(xb, packed1, heads, keep_rows)
+        project(xb, packed1, heads, factors1, keep_rows)
         wrapped = jnp.where(jnp.logical_and(last_lat, b == 3), 1.0, 0.0).astype(F32)
         rows = keep[1].astype(F32) * wrapped + (1.0 - wrapped)
         for p in range(2):
@@ -323,7 +333,7 @@
                 ctx[:, p, :, pl.ds(at, 128)] = value.reshape(2, 80, 128)
 
             mask = rows if p == 0 else rows * keep[0].astype(F32)
-            attend(fetch, keep_context, mask.astype(BF16), sides, scale1)
+            attend(fetch, keep_context, mask.astype(BF16), sides)
         branch = layer_norm(dot(ctx[...].reshape(320, 512), wout1[...]), gain1[...], offset1[...])
         result = (xb.astype(F32) + branch).reshape(2, 2, 80, 512)
         first[b] = result.astype(BF16)
@@ -348,6 +358,7 @@
     merge(1)
 
     second_loaded()
+    factors2 = head_scales(scale2)
     odd_half = odd.astype(F32)
     levels = keep[2].astype(F32) * odd_half + (1.0 - odd_half)
 
@@ -370,8 +381,8 @@
             mask = levels
         own = [quarter[cb, n].astype(F32) for n in range(4)]
         own = jnp.concatenate([jnp.concatenate([q[:ATOM], q[ATOM:]], axis=1) for q in own], axis=0)
-        project(own.astype(BF16), packed2, heads, keep_rows)
-        attend(fetch, keep_context, mask.astype(BF16), sides, scale2)
+        project(own.astype(BF16), packed2, heads, factors2, keep_rows)
+        attend(fetch, keep_context, mask.astype(BF16), sides)
         for half in (1, 0):
             branch = layer_norm(dot(ctx[0, half], wout2[...]), gain2[...], offset2[...])
             second = (own[80 * half : 80 * half + 80] + branch).astype(BF16)

time: 45.4 us -> 45.3 us (level)
  no operation moved by 1% of the time
where the time goes in v6:
time: 45.3 us; the launch traced here: 45.1 us
  Pallas kernels  42.7 us (94%)
  local copies, waits for them, and re-layouts  2.49 us (5%)
    pallas_call x1, Pallas kernels, body(): pl.pallas_call(functools.partial(kernel, nlat, nlon), out_shape=jax.Shape...  42.7 us
    pallas_call x1, local copies, waits for them, and re-layouts, body(): pl.pallas_call(functools.partial(kernel, nlat, nlon), out_shape=jax.Shape...  2.49 us

profile of v6, /device:TPU:1, one launch (start us, length us, event | category | flops | bytes accessed | tf_op | source)
XLA Modules:
  0.0 45.1 jit_solution(18243046865378973233)
XLA Ops:
  0.0 42.7 %shard_map.208 = bf16[2,144,1024]{2,1,0:T(8,128)(2,1)} custom-call(bf16[4,12,24,512]{3,2,1,0:T(8,128)(2,1)} %bitcast.12, bf16[512,1536]{1,0:T(8,128)(2,1)} %packed1_hbm.1, bf16[512,512]{1,0:T(8,128)(2,1)} %out1_hbm.1, bf16[2048,1024]{1,0:T(8,128)(2,1)} %merge_hbm.1, bf16[1024,1536]{1,0:T(8,128)(2,1)} %packed2_hbm.1, bf16[512,1024]{1,0:T(8,128)(2,1)} %out2_hbm.1, ...), custom_call_target="tpu_custom_call" | custom-call | flops 6000000000 | bytes 14000000 | tf_op jit(solution)/shard_map/pallas_call | solution.py:450
  42.7 2.5 %copy.24 = bf16[2,144,1024]{2,0,1:T(2,128)(2,1)} copy(bf16[2,144,1024]{2,1,0:T(8,128)(2,1)} %shard_map.208) | data formatting | bytes 1179648 | tf_op jit(solution)/shard_map/pallas_call | solution.py:450
